TPU v7x, 256 devices: a whole 4x4x8 slice. The times are simulated.
256 devices in a mesh: dp: 64 (over z, x, core), tp: 4 (over y).
Axes of the slice: x: 4, y: 4, z: 8, core: 2. Of those that a mesh axis runs over, the one named last changes fastest.
Arguments:
- hidden: bfloat16 [2048, 4096], P('dp', 'tp'), may hold values from -6 to 6
- routes: int32 [2048, 8], P('dp'), may hold values from 0 to 63, all different within a row; in each aligned block of 32 rows (0 to 31, 32 to 63, ...) at most 8 rows name the same one
- routing_weights: float32 [2048, 8], P('dp'), may hold values from 0.05 to 1
- w_gate: bfloat16 [64, 4096, 1536], P('dp', None, 'tp'), may hold values from -0.09375 to 0.09375
- w_up: bfloat16 [64, 4096, 1536], P('dp', None, 'tp'), may hold values from -0.09375 to 0.09375
- w_down: bfloat16 [64, 1536, 4096], P('dp', 'tp'), may hold values from -0.15625 to 0.15625
- norm_gain: float32 [4096], replicated, may hold values from 0.1 to 1.9
- key_projection_weight: bfloat16 [4096, 512], P(None, 'tp'), may hold values from -0.09375 to 0.09375
- value_projection_weight: bfloat16 [4096, 512], P(None, 'tp'), may hold values from -0.09375 to 0.09375
- queries: bfloat16 [2048, 8192], P('dp', 'tp'), may hold values from -128 to 128
- cached_key_rows: bfloat16 [64, 128, 512], P('dp', None, 'tp'), may hold values from -4 to 4
- cached_value_rows: bfloat16 [64, 128, 512], P('dp', None, 'tp'), may hold values from -6 to 6
- lengths: int32 [64], P('dp'), may hold values from 16 to 128
- parents: int32 [64, 32], P('dp'), may hold values from -1 to 30, as said below
Outputs:
- layer_output: bfloat16 [2048, 4096], P('dp', 'tp')
- next_layer_keys: bfloat16 [2048, 512], P('dp', 'tp')
- next_layer_values: bfloat16 [2048, 512], P('dp', 'tp')
- attended: bfloat16 [2048, 8192], P('dp', 'tp')
Inputs may be any that keep to these rules, and one draw needn't show every extreme that they name: `routes`: each row names 8 different experts. In each aligned block of 32 rows (the rows of one device) no expert is named by more than 8 rows, a bound that some block reaches. `parents`: node 0 of each request is the root, with parent -1; every other node i has its parent among nodes max(0, i - 8) to i - 1.
All inputs are finite; a program needn't handle non-finite values.
Results may differ from a plain program's by a relative error of at most 0.013.
Values may be sent and summed in bfloat16 or wider, within the bound.
No kernel may reach another device: no remote copies, remote signals or barrier semaphores. Data moves between devices by JAX's collectives and lax.ppermute only.
A program may use at most 64 MiB of HBM per device.

v0:
```python
import math

import jax
import jax.numpy as jnp
from jax import lax
from jax.sharding import PartitionSpec as P

HEAD_SIZE = 128


def split_up(shard, dim, size):
    shape = shard.shape
    tiles = shard.reshape(*shape[:dim], size, shape[dim] // size, *shape[dim + 1 :])
    return jnp.moveaxis(tiles, dim, 0)


def sent_and_summed(shard, axis, dim):
    size = lax.axis_size(axis)
    tiles = lax.all_to_all(split_up(shard, dim, size), axis, 0, 0, tiled=True)
    return jnp.sum(tiles.astype(jnp.float32), axis=0)


def joined_along(tiles, dim):
    shape = list(tiles.shape[1:])
    shape[dim] *= tiles.shape[0]
    return jnp.moveaxis(tiles, 0, dim).reshape(shape)


def copy_for_each(shard, axis):
    copies = jnp.broadcast_to(shard, (lax.axis_size(axis), *shard.shape))
    return lax.all_to_all(copies, axis, split_axis=0, concat_axis=0, tiled=True)


def gathered_copies(shard, axis, dim):
    return joined_along(copy_for_each(shard, axis), dim)


def ancestry(parent_row):
    node_count = parent_row.shape[0]
    position = jnp.arange(node_count, dtype=jnp.int32)
    reached = (parent_row[:, None] == position[None, :]).astype(jnp.float32)
    reached = reached + jnp.eye(node_count, dtype=jnp.float32)
    for doubling in range((node_count - 1).bit_length()):
        reached = jnp.minimum(jnp.dot(reached, reached, preferred_element_type=jnp.float32), 1.0)
    return reached > 0.5


def quarter_to_whole(received):
    return lax.all_gather(received, "tp", axis=2, tiled=True)


def attend_local(
    queries, cached_key_rows, cached_value_rows, tree_key_rows, tree_value_rows, lengths, parents
):
    request_count = lengths.shape[0]
    node_count = parents.shape[1]
    slot_length = cached_key_rows.shape[1]
    kv_local = cached_key_rows.shape[2] // HEAD_SIZE
    query_group_count = queries.shape[1] // (kv_local * HEAD_SIZE)
    scaled = 1.0 / math.sqrt(HEAD_SIZE)
    tree_query_block = queries.reshape(
        request_count, node_count, kv_local, query_group_count, HEAD_SIZE
    )
    joined_key_block = cached_key_rows.reshape(request_count, slot_length, kv_local, HEAD_SIZE)
    joined_value_block = cached_value_rows.reshape(request_count, slot_length, kv_local, HEAD_SIZE)
    tree_key_block = tree_key_rows.reshape(request_count, node_count, kv_local, HEAD_SIZE)
    tree_value_block = tree_value_rows.reshape(request_count, node_count, kv_local, HEAD_SIZE)
    cache_scores = (
        jnp.einsum(
            "rnkgd,rpkd->rkgnp",
            tree_query_block,
            joined_key_block,
            preferred_element_type=jnp.float32,
        )
        * scaled
    )
    tree_scores = (
        jnp.einsum(
            "rnkgd,rmkd->rkgnm",
            tree_query_block,
            tree_key_block,
            preferred_element_type=jnp.float32,
        )
        * scaled
    )
    visible = jnp.arange(slot_length, dtype=jnp.int32)[None, :] < lengths[:, None]
    cache_scores = jnp.where(visible[:, None, None, None, :], cache_scores, -1e30)
    related = jax.vmap(ancestry)(parents)
    tree_scores = jnp.where(related[:, None, None], tree_scores, -1e30)
    highest = jnp.maximum(jnp.max(cache_scores, axis=-1), jnp.max(tree_scores, axis=-1))[..., None]
    cache_raised = jnp.exp(cache_scores - highest)
    tree_raised = jnp.exp(tree_scores - highest)
    denominator = jnp.sum(cache_raised, axis=-1, keepdims=True) + jnp.sum(
        tree_raised, axis=-1, keepdims=True
    )
    cache_weights = (cache_raised / denominator).astype(jnp.bfloat16)
    tree_weights = (tree_raised / denominator).astype(jnp.bfloat16)
    output = jnp.einsum(
        "rkgnp,rpkd->rnkgd", cache_weights, joined_value_block, preferred_element_type=jnp.float32
    )
    output = output + jnp.einsum(
        "rkgnm,rmkd->rnkgd", tree_weights, tree_value_block, preferred_element_type=jnp.float32
    )
    return output.reshape(request_count * node_count, -1).astype(jnp.bfloat16)


def on_device(
    hidden,
    routes,
    routing_weights,
    w_gate,
    w_up,
    w_down,
    norm_gain,
    key_projection_weight,
    value_projection_weight,
    queries,
    cached_key_rows,
    cached_value_rows,
    lengths,
    parents,
):
    token_count = hidden.shape[0]
    top_count = routes.shape[1]
    local_experts = w_gate.shape[0]
    expert_count = lax.axis_size("dp") * local_experts
    capacity = min(token_count, 2 * token_count * top_count // expert_count)
    column_count = hidden.shape[1]
    weights = routing_weights / jnp.sum(routing_weights, axis=1, keepdims=True)
    expert_ids = jnp.arange(expert_count, dtype=jnp.int32)
    chosen = routes[:, :, None] == expert_ids[None, None, :]
    member = jnp.any(chosen, axis=1)
    portion = jnp.sum(jnp.where(chosen, weights[:, :, None], 0.0), axis=1)
    earlier = jnp.tril(jnp.ones((token_count, token_count), jnp.bfloat16), -1)
    rank = jnp.dot(earlier, member.astype(jnp.bfloat16), preferred_element_type=jnp.float32)
    slots = jnp.arange(capacity, dtype=jnp.float32)
    placed = member.T[:, None, :] & (rank.T[:, None, :] == slots[None, :, None])
    placed = placed.reshape(expert_count * capacity, token_count)
    outgoing = jnp.dot(
        placed.astype(jnp.bfloat16), hidden, preferred_element_type=jnp.float32
    ).astype(jnp.bfloat16)
    outgoing = outgoing.reshape(expert_count, capacity, column_count)
    received = quarter_to_whole(
        lax.all_to_all(outgoing, "dp", split_axis=0, concat_axis=0, tiled=True)
    )
    slot_count = received.shape[1]
    grouped = received.reshape(-1, local_experts, slot_count, received.shape[2])
    gate_act = jnp.einsum("secd,edf->secf", grouped, w_gate, preferred_element_type=jnp.float32)
    upward = jnp.einsum("secd,edf->secf", grouped, w_up, preferred_element_type=jnp.float32)
    active = (jax.nn.silu(gate_act) * upward).astype(jnp.bfloat16)
    partial_value = jnp.einsum("secf,efd->secd", active, w_down, preferred_element_type=jnp.float32)
    partial_value = partial_value.reshape(received.shape[0], slot_count, partial_value.shape[3])
    summed = sent_and_summed(partial_value.astype(jnp.bfloat16), "tp", 2)
    back = lax.all_to_all(
        summed.astype(jnp.bfloat16), "dp", split_axis=0, concat_axis=0, tiled=True
    )
    flat_back = back.reshape(expert_count * capacity, back.shape[2])
    spread = jnp.broadcast_to(portion.T[:, None, :], (expert_count, capacity, token_count))
    spread = jnp.where(placed, spread.reshape(expert_count * capacity, token_count), 0.0)
    upper = spread.astype(jnp.bfloat16)
    lower = (spread - upper.astype(jnp.float32)).astype(jnp.bfloat16)
    both = jnp.concatenate([upper, lower], axis=1)
    mixed = lax.dot_general(
        both, flat_back, (((0,), (0,)), ((), ())), preferred_element_type=jnp.float32
    )
    expert_mix = mixed[:token_count] + mixed[token_count:]
    own_out = (hidden.astype(jnp.float32) + expert_mix).astype(jnp.bfloat16)
    full_out = gathered_copies(own_out, "tp", 1)
    widened = full_out.astype(jnp.float32)
    scaling = lax.rsqrt(jnp.mean(widened * widened, axis=1, keepdims=True) + 1e-06)
    normed = (widened * scaling * norm_gain).astype(jnp.bfloat16)
    tree_key_rows = jnp.dot(
        normed, key_projection_weight, preferred_element_type=jnp.float32
    ).astype(jnp.bfloat16)
    tree_value_rows = jnp.dot(
        normed, value_projection_weight, preferred_element_type=jnp.float32
    ).astype(jnp.bfloat16)
    attended = attend_local(
        queries,
        cached_key_rows,
        cached_value_rows,
        tree_key_rows,
        tree_value_rows,
        lengths,
        parents,
    )
    return (own_out, tree_key_rows, tree_value_rows, attended)


def solution(mesh):
    return jax.shard_map(
        on_device,
        mesh=mesh,
        in_specs=(
            P("dp", "tp"),
            P("dp", None),
            P("dp", None),
            P("dp", None, "tp"),
            P("dp", None, "tp"),
            P("dp", "tp", None),
            P(),
            P(None, "tp"),
            P(None, "tp"),
            P("dp", "tp"),
            P("dp", None, "tp"),
            P("dp", None, "tp"),
            P("dp"),
            P("dp", None),
        ),
        out_specs=(P("dp", "tp"), P("dp", "tp"), P("dp", "tp"), P("dp", "tp")),
        check_vma=False,
    )
```

profile of v0, /device:TPU:2, one launch (start us, length us, event | category | flops | bytes accessed | tf_op | source)
XLA Modules:
  0.0 239.4 jit_solution(4586139410621288270)
XLA Ops:
  7.2 0.0 copy-start
  7.2 0.0 all-gather.2.cloned.1.call-start
  7.2 0.9 copy.67
  8.2 0.7 reduce_sum.57
  8.9 0.7 broadcast_divide_fusion
  9.5 0.1 copy.72
  9.6 0.1 fusion.45
  9.8 0.1 select_reduce_fusion
  9.9 0.1 copy.73
  10.0 0.1 copy.74
  10.1 0.2 fusion.55
  10.3 0.1 copy.70
  10.5 0.1 copy.68
  10.6 0.1 copy.71
  10.7 0.1 eq.96
  10.9 1.3 fusion.5
  12.2 40.7 %all_to_all.20 = bf16[64,8,1024]{2,1,0:T(8,128)(2,1)} all-to-all(bf16[64,8,1024]{2,1,0:T(8,128)(2,1)S(1)} %fusion.5), channel_id=1, replica_groups=mesh['dp'=64,'tp'=4] {'dp'}, dimensions={0} | all-to-all | bytes 2097152 | tf_op jit(solution)/shard_map/all_to_all | solution.py:144
  52.9 0.0 all-gather.2.cloned.1.call-update
  52.9 47.6 %all-gather.2.cloned.1.call-done = bf16[64,8,4096]{2,1,0:T(8,128)(2,1)} async-done(((bf16[64,8,1024]{2,1,0:T(8,128)(2,1)}), bf16[64,8,4096]{2,1,0:T(8,128)(2,1)}) %all-gather.2.cloned.1.call-update) | async-done | bytes 4194320 | tf_op jit(solution)/shard_map/all_gather | solution.py:49
  100.5 6.4 %fusion.6 = f32[64,1,8,384]{3,2,0,1:T(8,128)} fusion(bf16[64,8,4096]{2,1,0:T(8,128)(2,1)} %all-gather.2.cloned.1.call-done, bf16[1,4096,384]{2,1,0:T(8,128)(2,1)} %param.17), kind=kOutput, calls=%fused_computation.9 | convolution fusion | flops 1610612736 | bytes 8126464 | tf_op jit(solution)/shard_map/secd,edf->secf/dot_general | solution.py:148
  107.0 9.7 %convolution_convert_fusion = bf16[64,8,4096]{2,1,0:T(8,128)(2,1)} fusion(bf16[1,384,4096]{2,1,0:T(8,128)(2,1)S(1)} %copy-done, bf16[64,8,4096]{2,1,0:T(8,128)(2,1)} %all-gather.2.cloned.1.call-done, bf16[1,4096,384]{2,1,0:T(8,128)(2,1)} %param.18, f32[64,1,8,384]{3,2,0,1:T(8,128)} %fusion.6), kind=kOutput, calls=%fused_computation | convolution fusion | flops 3224502272 | bytes 15466496 | tf_op jit(solution)/shard_map/secf,efd->secd/dot_general | solution.py:151
  116.7 2.6 %copy.101 = bf16[64,8,4,1024]{3,1,0,2:T(8,128)(2,1)S(1)} copy(bf16[64,8,4,1024]{3,1,2,0:T(8,128)(2,1)} %bitcast.160) | data formatting | bytes 8388608 | tf_op jit(solution)/shard_map/convert_element_type | solution.py:153
  119.3 52.5 %all_to_all.21 = bf16[4,64,8,1024]{3,2,1,0:T(8,128)(2,1)} all-to-all(bf16[4,64,8,1024]{3,2,1,0:T(8,128)(2,1)S(1)} %bitcast.157), channel_id=1, replica_groups=mesh['dp'=64,'tp'=4] {'tp'}, dimensions={0} | all-to-all | bytes 8388608 | tf_op jit(solution)/shard_map/all_to_all | solution.py:19
  171.8 4.4 %reduce_sum.59 = bf16[64,8,1024]{2,1,0:T(8,128)(2,1)} reduce(bf16[4,64,8,1024]{3,2,1,0:T(8,128)(2,1)} %all_to_all.21, bf16[]{:T(256)} %constant.15.clone.1), dimensions={0}, to_apply=%region_3.4 | reduce | flops 1572864 | bytes 5242882 | tf_op jit(solution)/shard_map/reduce_sum | solution.py:20
  176.2 10.8 %all-to-all-start.2 = ((bf16[64,8,1024]{2,1,0:T(8,128)(2,1)}), bf16[64,8,1024]{2,1,0:T(8,128)(2,1)}, u32[]{:S(2)}, u32[]{:S(2)}) async-start(bf16[64,8,1024]{2,1,0:T(8,128)(2,1)} %reduce_sum.59), calls=%async_computation.2 | async-start | bytes 2097152 | tf_op jit(solution)/shard_map/all_to_all | solution.py:154
  187.1 0.1 fusion.53
  187.2 0.1 convolution_minimum_fusion.4
  187.3 0.2 convolution_minimum_fusion.2
  187.5 0.2 fusion.28
  187.8 0.7 copy.78
  189.1 0.5 iota_compare_fusion.2
  189.7 26.1 %all-to-all-done.2 = bf16[64,8,1024]{2,1,0:T(8,128)(2,1)} async-done(((bf16[64,8,1024]{2,1,0:T(8,128)(2,1)}), bf16[64,8,1024]{2,1,0:T(8,128)(2,1)}, u32[]{:S(2)}, u32[]{:S(2)}) %all-to-all-start.2) | async-done | bytes 1048608 | tf_op jit(solution)/shard_map/all_to_all | solution.py:154
  215.8 1.6 fusion.29
  217.4 0.0 copy-start.5
  217.4 0.7 broadcast_in_dim.81
  218.1 3.4 %all-to-all-start.3 = ((bf16[4,32,1024]{2,1,0:T(8,128)(2,1)}), bf16[4,32,1024]{2,1,0:T(8,128)(2,1)S(1)}, u32[]{:S(2)}, u32[]{:S(2)}) async-start(bf16[4,32,1024]{2,1,0:T(8,128)(2,1)} %broadcast_in_dim.81), calls=%async_computation.3 | async-start | bytes 524288 | tf_op jit(solution)/shard_map/all_to_all | solution.py:31
  221.5 2.4 %fusion.71 = (f32[16,32]{1,0:T(8,128)}, f32[1,1,16,32,128]{4,3,2,1,0:T(8,128)}) fusion(bf16[1,128,128]{2,1,0:T(8,128)(2,1)} %param.24, pred[128]{0:T(512)(128)(4,1)} %iota_compare_fusion.2, bf16[32,2048]{1,0:T(8,128)(2,1)} %param.23), kind=kOutput, calls=%fused_computation.96 | convolution fusion | flops 16973312 | bytes 428160 | tf_op jit(solution)/shard_map/rnkgd,rpkd->rkgnp/dot_general | solution.py:69
  223.9 4.2 %all-to-all-done.3 = bf16[4,32,1024]{2,1,0:T(8,128)(2,1)S(1)} async-done(((bf16[4,32,1024]{2,1,0:T(8,128)(2,1)}), bf16[4,32,1024]{2,1,0:T(8,128)(2,1)S(1)}, u32[]{:S(2)}, u32[]{:S(2)}) %all-to-all-start.3) | async-done | bytes 262176 | tf_op jit(solution)/shard_map/all_to_all | solution.py:31
  228.3 0.2 fusion.33
  228.5 1.7 convolution_convert_fusion.3
  230.2 0.3 fusion.72
  230.5 0.1 fusion.36
  230.6 0.3 fusion.35
  230.9 0.3 convolution_convert_fusion.2
  231.3 0.3 convolution_bitcast_fusion
  231.6 0.3 fusion.27
  231.8 0.1 copy.81
  231.9 0.7 copy.102
  (37 shorter events, 0.3 us)
Async XLA Ops:
  7.2 99.8 %copy-start = (bf16[1,384,4096]{2,1,0:T(8,128)(2,1)S(1)}, bf16[1,384,4096]{2,1,0:T(8,128)(2,1)}, u32[]{:S(2)}) copy-start(bf16[1,384,4096]{2,1,0:T(8,128)(2,1)} %param.19) | copy-start | bytes 9437188
  7.2 93.3 %all-gather.2.cloned.1.call-start = ((), (), s32[]{:S(2)}) async-start(), calls=%async_computation.4 | async-start | bytes 5242880 | tf_op jit(solution)/shard_map/all_gather | solution.py:49
  171.8 15.3 %copy-start.11 = (s32[1,32]{1,0:T(1,128)S(1)}, s32[1,32]{1,0:T(1,128)}, u32[]{:S(2)}) copy-start(s32[1,32]{1,0:T(1,128)} %param.27) | copy-start | bytes 388
  176.2 41.1 %copy-start.4 = (bf16[32,1024]{1,0:T(8,128)(2,1)S(1)}, bf16[32,1024]{1,0:T(8,128)(2,1)}, u32[]{:S(2)}) copy-start(bf16[32,1024]{1,0:T(8,128)(2,1)} %param.14) | copy-start | bytes 196612
  176.2 39.6 %all-to-all-start.2 = ((bf16[64,8,1024]{2,1,0:T(8,128)(2,1)}), bf16[64,8,1024]{2,1,0:T(8,128)(2,1)}, u32[]{:S(2)}, u32[]{:S(2)}) async-start(bf16[64,8,1024]{2,1,0:T(8,128)(2,1)} %reduce_sum.59), calls=%async_computation.2 | async-start | bytes 2097152 | tf_op jit(solution)/shard_map/all_to_all | solution.py:154
  187.0 41.4 %copy-start.6 = (f32[4096]{0:T(1024)S(1)}, f32[4096]{0:T(1024)}, u32[]{:S(2)}) copy-start(f32[4096]{0:T(1024)} %param.20) | copy-start | bytes 49156
  215.8 14.4 %copy-start.3 = (bf16[32,2048]{1,0:T(8,128)(2,1)S(1)}, bf16[32,2048]{1,0:T(8,128)(2,1)}, u32[]{:S(2)}) copy-start(bf16[32,2048]{1,0:T(8,128)(2,1)} %param.23) | copy-start | bytes 393220
  217.4 0.7 copy-start.5
  218.1 10.1 %all-to-all-start.3 = ((bf16[4,32,1024]{2,1,0:T(8,128)(2,1)}), bf16[4,32,1024]{2,1,0:T(8,128)(2,1)S(1)}, u32[]{:S(2)}, u32[]{:S(2)}) async-start(bf16[4,32,1024]{2,1,0:T(8,128)(2,1)} %broadcast_in_dim.81), calls=%async_computation.3 | async-start | bytes 524288 | tf_op jit(solution)/shard_map/all_to_all | solution.py:31
  228.2 2.0 copy-start.9
  228.2 2.4 copy-start.8
  228.2 2.5 %copy-start.2 = (f32[1,1,16,32,128]{4,3,2,1,0:T(8,128)S(1)}, f32[1,1,16,32,128]{4,3,2,1,0:T(8,128)}, u32[]{:S(2)}) copy-start(f32[1,1,16,32,128]{4,3,2,1,0:T(8,128)} %get-tuple-element.7) | copy-start | bytes 786436
  228.2 2.7 %copy-start.1 = (bf16[4096,128]{1,0:T(8,128)(2,1)S(1)}, bf16[4096,128]{1,0:T(8,128)(2,1)}, u32[]{:S(2)}) copy-start(bf16[4096,128]{1,0:T(8,128)(2,1)} %param.22) | copy-start | bytes 3145732
  228.2 3.1 %copy-start.12 = (bf16[1,128,128]{2,1,0:T(8,128)(2,1)S(1)}, bf16[1,128,128]{2,1,0:T(8,128)(2,1)}, u32[]{:S(2)}) copy-start(bf16[1,128,128]{2,1,0:T(8,128)(2,1)} %param.25) | copy-start | bytes 98308
  230.2 2.4 %copy-start.7 = (bf16[32,128]{1,0:T(8,128)(2,1)}, bf16[32,128]{1,0:T(8,128)(2,1)S(1)}, u32[]{:S(2)}) copy-start(bf16[32,128]{1,0:T(8,128)(2,1)S(1)} %convolution_convert_fusion.3) | copy-start | bytes 24580
  231.2 1.4 copy-start.10
Sparse Core Ops, SparseCore 0:
  53.0 47.4 all-gather.1
where the time goes:
time: 240 us; the launch traced here: 239 us
  blocking collectives  93.2 us (39%)
  waiting for transfers between devices  77.9 us (32%)
  matrix products  25.2 us (10%)
  between operations  15 us (6%)
  starting transfers between devices  14.3 us (6%)
  other arithmetic  7.3 us (3%)
  local copies, waits for them, and re-layouts  6.57 us (3%)
    all_to_all x1, blocking collectives, sent_and_summed(): tiles = lax.all_to_all(split_up(shard, dim, size), axis, 0, 0, tiled=True)  52.5 us
    all_gather x1, waiting for transfers between devices, quarter_to_whole(): return lax.all_gather(received, 'tp', axis=2, tiled=True)  47.6 us
    all_to_all x1, blocking collectives, on_device(): lax.all_to_all(outgoing, 'dp', split_axis=0, concat_axis=0, tiled=True)  40.7 us
    all_to_all x1, waiting for transfers between devices, on_device(): lax.all_to_all(summed.astype(jnp.bfloat16), 'dp', split_axis=0, concat_ax...  26.1 us
    all_to_all x1, starting transfers between devices, on_device(): lax.all_to_all(summed.astype(jnp.bfloat16), 'dp', split_axis=0, concat_ax...  10.8 us
    dot_general x1, matrix products, on_device(): jnp.einsum('secf,efd->secd', active, w_down, preferred_element_type=jnp.f...  9.74 us
    dot_general x1, matrix products, on_device(): jnp.einsum('secd,edf->secf', grouped, w_gate, preferred_element_type=jnp....  6.43 us
  transfers between devices with their start and end apart: 3, of which 3 were waited for; matrix products, arithmetic and copies ran while one was open for 2% of the time, Pallas kernels for 0%

commit v1 on v0

--- a/solution.py
+++ b/solution.py
@@ -3,21 +3,45 @@
 import jax
 import jax.numpy as jnp
 from jax import lax
+from jax.experimental import pallas as pl
 from jax.sharding import PartitionSpec as P
 
 HEAD_SIZE = 128
-
-
-def split_up(shard, dim, size):
-    shape = shard.shape
-    tiles = shard.reshape(*shape[:dim], size, shape[dim] // size, *shape[dim + 1 :])
-    return jnp.moveaxis(tiles, dim, 0)
-
-
-def sent_and_summed(shard, axis, dim):
-    size = lax.axis_size(axis)
-    tiles = lax.all_to_all(split_up(shard, dim, size), axis, 0, 0, tiled=True)
-    return jnp.sum(tiles.astype(jnp.float32), axis=0)
+CHUNKS = 1
+
+
+def shifted(value, step):
+    size = lax.axis_size("tp")
+    return lax.ppermute(value, "tp", [(i, (i + step) % size) for i in range(size)])
+
+
+def gathered_ring(rows):
+    half = rows.shape[0] // 2
+    before = shifted(rows, 1)
+    after = shifted(rows, -1)
+    opposite = jnp.concatenate([shifted(before[:half], 1), shifted(after[half:], -1)], axis=0)
+    return rows, before, after, opposite
+
+
+def around(value, dim, size):
+    index = lax.axis_index("tp")
+    count = lax.axis_size("tp")
+    return [
+        lax.dynamic_slice_in_dim(value, ((index + step) % count) * size, size, dim)
+        for step in (0, count - 1, 1, 2)
+    ]
+
+
+def sent_around(blocks):
+    to_before, to_after, to_opposite = blocks
+    return shifted(to_after, 1), shifted(to_before, -1), shifted(to_opposite, 2)
+
+
+def summed_products(blocks, weights):
+    total = jnp.dot(blocks[0], weights[0], preferred_element_type=jnp.float32)
+    for block, weight in zip(blocks[1:], weights[1:]):
+        total = total + jnp.dot(block, weight, preferred_element_type=jnp.float32)
+    return total
 
 
 def joined_along(tiles, dim):
@@ -35,25 +59,31 @@
     return joined_along(copy_for_each(shard, axis), dim)
 
 
-def ancestry(parent_row):
-    node_count = parent_row.shape[0]
-    position = jnp.arange(node_count, dtype=jnp.int32)
-    reached = (parent_row[:, None] == position[None, :]).astype(jnp.float32)
-    reached = reached + jnp.eye(node_count, dtype=jnp.float32)
+def ancestry_kernel(parents_ref, related_ref):
+    node_count = parents_ref.shape[0]
+    column = lax.broadcasted_iota(jnp.int32, (node_count, node_count), 1)
+    row = lax.broadcasted_iota(jnp.int32, (node_count, node_count), 0)
+    reached = jnp.where((parents_ref[...] == column) | (row == column), 1.0, 0.0)
     for doubling in range((node_count - 1).bit_length()):
-        reached = jnp.minimum(jnp.dot(reached, reached, preferred_element_type=jnp.float32), 1.0)
-    return reached > 0.5
-
-
-def quarter_to_whole(received):
-    return lax.all_gather(received, "tp", axis=2, tiled=True)
+        product = jnp.dot(reached, reached, preferred_element_type=jnp.float32)
+        reached = jnp.minimum(product, 1.0)
+    related_ref[...] = reached
+
+
+def ancestry(parents):
+    node_count = parents.shape[1]
+    return pl.pallas_call(
+        ancestry_kernel,
+        out_shape=jax.ShapeDtypeStruct((node_count, node_count), jnp.float32),
+        cost_estimate=pl.CostEstimate(flops=23070000000, bytes_accessed=8192, transcendentals=0),
+    )(parents.reshape(node_count, 1))
 
 
 def attend_local(
-    queries, cached_key_rows, cached_value_rows, tree_key_rows, tree_value_rows, lengths, parents
+    queries, cached_key_rows, cached_value_rows, tree_key_rows, tree_value_rows, lengths, related
 ):
     request_count = lengths.shape[0]
-    node_count = parents.shape[1]
+    node_count = related.shape[0]
     slot_length = cached_key_rows.shape[1]
     kv_local = cached_key_rows.shape[2] // HEAD_SIZE
     query_group_count = queries.shape[1] // (kv_local * HEAD_SIZE)
@@ -85,8 +115,7 @@
     )
     visible = jnp.arange(slot_length, dtype=jnp.int32)[None, :] < lengths[:, None]
     cache_scores = jnp.where(visible[:, None, None, None, :], cache_scores, -1e30)
-    related = jax.vmap(ancestry)(parents)
-    tree_scores = jnp.where(related[:, None, None], tree_scores, -1e30)
+    tree_scores = jnp.where(related[None, None, None] > 0.5, tree_scores, -1e30)
     highest = jnp.maximum(jnp.max(cache_scores, axis=-1), jnp.max(tree_scores, axis=-1))[..., None]
     cache_raised = jnp.exp(cache_scores - highest)
     tree_raised = jnp.exp(tree_scores - highest)
@@ -122,10 +151,11 @@
 ):
     token_count = hidden.shape[0]
     top_count = routes.shape[1]
-    local_experts = w_gate.shape[0]
-    expert_count = lax.axis_size("dp") * local_experts
+    expert_count = lax.axis_size("dp")
     capacity = min(token_count, 2 * token_count * top_count // expert_count)
     column_count = hidden.shape[1]
+    down_own, *down_sent = around(w_down[0], 1, column_count)
+    routes, routing_weights, down_sent = lax.optimization_barrier((routes, routing_weights, down_sent))
     weights = routing_weights / jnp.sum(routing_weights, axis=1, keepdims=True)
     expert_ids = jnp.arange(expert_count, dtype=jnp.int32)
     chosen = routes[:, :, None] == expert_ids[None, None, :]
@@ -140,21 +170,33 @@
         placed.astype(jnp.bfloat16), hidden, preferred_element_type=jnp.float32
     ).astype(jnp.bfloat16)
     outgoing = outgoing.reshape(expert_count, capacity, column_count)
-    received = quarter_to_whole(
-        lax.all_to_all(outgoing, "dp", split_axis=0, concat_axis=0, tiled=True)
-    )
-    slot_count = received.shape[1]
-    grouped = received.reshape(-1, local_experts, slot_count, received.shape[2])
-    gate_act = jnp.einsum("secd,edf->secf", grouped, w_gate, preferred_element_type=jnp.float32)
-    upward = jnp.einsum("secd,edf->secf", grouped, w_up, preferred_element_type=jnp.float32)
-    active = (jax.nn.silu(gate_act) * upward).astype(jnp.bfloat16)
-    partial_value = jnp.einsum("secf,efd->secd", active, w_down, preferred_element_type=jnp.float32)
-    partial_value = partial_value.reshape(received.shape[0], slot_count, partial_value.shape[3])
-    summed = sent_and_summed(partial_value.astype(jnp.bfloat16), "tp", 2)
-    back = lax.all_to_all(
-        summed.astype(jnp.bfloat16), "dp", split_axis=0, concat_axis=0, tiled=True
-    )
-    flat_back = back.reshape(expert_count * capacity, back.shape[2])
+    down_received = sent_around(down_sent)
+    down_received, parents = lax.optimization_barrier((down_received, parents))
+    related = ancestry(parents)
+    down_blocks = [down_own, *down_received]
+    hidden_units = w_gate.shape[2]
+    both_weights = [
+        jnp.concatenate(pair, axis=1)
+        for pair in zip(around(w_gate[0], 0, column_count), around(w_up[0], 0, column_count))
+    ]
+    received = lax.all_to_all(outgoing, "dp", split_axis=0, concat_axis=0, tiled=True)
+    received, down_blocks, both_weights, related = lax.optimization_barrier(
+        (received, down_blocks, both_weights, related)
+    )
+    chunk = capacity // CHUNKS
+    returned = []
+    for part in range(CHUNKS):
+        rows = received[:, part * chunk : (part + 1) * chunk].reshape(expert_count * chunk, column_count)
+        products = summed_products(gathered_ring(rows), both_weights)
+        gate_act, upward = products[:, :hidden_units], products[:, hidden_units:]
+        active = (jax.nn.silu(gate_act) * upward).astype(jnp.bfloat16)
+        made = summed_products(gathered_ring(active), down_blocks).astype(jnp.bfloat16)
+        returned.append(
+            lax.all_to_all(
+                made.reshape(expert_count, chunk, column_count), "dp", split_axis=0, concat_axis=0, tiled=True
+            )
+        )
+    flat_back = jnp.concatenate(returned, axis=1).reshape(expert_count * capacity, column_count)
     spread = jnp.broadcast_to(portion.T[:, None, :], (expert_count, capacity, token_count))
     spread = jnp.where(placed, spread.reshape(expert_count * capacity, token_count), 0.0)
     upper = spread.astype(jnp.bfloat16)
@@ -182,7 +224,7 @@
         tree_key_rows,
         tree_value_rows,
         lengths,
-        parents,
+        related,
     )
     return (own_out, tree_key_rows, tree_value_rows, attended)
 

time: 240 us -> 169 us (0.70)
  blocking collectives: 93.2 us -> 0 us
  starting transfers between devices: 14.3 us -> 44.1 us
  between operations: 15 us -> 1.84 us
  waiting for transfers between devices: 77.9 us -> 87.3 us
  matrix products: 25.2 us -> 16.7 us
  local copies, waits for them, and re-layouts: 6.57 us -> 10.9 us
    all_to_all x2 -> x0, blocking collectives: 93.2 us -> none  [the longest x1 52.5 us: sent_and_summed(): tiles = lax.all_to_all(split_up(shard, dim, size), axis, 0, 0, tiled=True)]
    all_gather x1 -> x0, waiting for transfers between devices: 47.6 us -> none  [quarter_to_whole(): return lax.all_gather(received, 'tp', axis=2, tiled=True)]
    ppermute x0 -> x11, waiting for transfers between devices: none -> 45.6 us  [shifted(): lax.ppermute(value, 'tp', [(i, (i + step) % size) for i in range(size)])]
    ppermute x0 -> x11, starting transfers between devices: none -> 19.2 us  [shifted(): lax.ppermute(value, 'tp', [(i, (i + step) % size) for i in range(size)])]
    all_to_all x1 -> x2, starting transfers between devices: 10.8 us -> 21.5 us  [the longest x1 12.2 us: on_device(): lax.all_to_all(outgoing, 'dp', split_axis=0, concat_axis=0, tiled=True)]
    all_to_all x1 -> x2, waiting for transfers between devices: 26.1 us -> 35.2 us  [the longest x1 27.8 us: on_device(): lax.all_to_all(made.reshape(expert_count, chunk, column_count), 'dp', spl...]
    dynamic_slice x0 -> x2, local copies, waits for them, and re-layouts: none -> 6.87 us  [around(): lax.dynamic_slice_in_dim(value, (index + step) % count * size, size, dim)]
    reduce_sum x1 -> x0, other arithmetic: 4.39 us -> none  [sent_and_summed(): return jnp.sum(tiles.astype(jnp.float32), axis=0)]
  transfers between devices with their start and end apart: 3 -> 14, of which waited for: 3 -> 9; matrix products, arithmetic and copies ran while one was open for 2% -> 13% of each run, Pallas kernels for 0% -> 1%
where the time goes in v1:
time: 169 us
  waiting for transfers between devices  87.3 us (52%)
  starting transfers between devices  44.1 us (26%)
  matrix products  16.7 us (10%)
  local copies, waits for them, and re-layouts  10.9 us (6%)
  other arithmetic  5.75 us (3%)
  Pallas kernels  1.98 us (1%)
  between operations  1.84 us (1%)
    ppermute x11, waiting for transfers between devices, shifted(): lax.ppermute(value, 'tp', [(i, (i + step) % size) for i in range(size)])  45.6 us
    all_to_all x1, waiting for transfers between devices, on_device(): lax.all_to_all(made.reshape(expert_count, chunk, column_count), 'dp', spl...  27.8 us
    ppermute x11, starting transfers between devices, shifted(): lax.ppermute(value, 'tp', [(i, (i + step) % size) for i in range(size)])  19.2 us
    all_to_all x1, starting transfers between devices, on_device(): lax.all_to_all(outgoing, 'dp', split_axis=0, concat_axis=0, tiled=True)  12.2 us
    dot_general x6, matrix products, summed_products(): total = total + jnp.dot(block, weight, preferred_element_type=jnp.float32)  9.52 us
    all_to_all x1, starting transfers between devices, on_device(): lax.all_to_all(made.reshape(expert_count, chunk, column_count), 'dp', spl...  9.29 us
    all_to_all x1, waiting for transfers between devices, on_device(): lax.all_to_all(outgoing, 'dp', split_axis=0, concat_axis=0, tiled=True)  7.43 us
    dynamic_slice x2, local copies, waits for them, and re-layouts, around(): lax.dynamic_slice_in_dim(value, (index + step) % count * size, size, dim)  6.87 us
  transfers between devices with their start and end apart: 14, of which 9 were waited for; matrix products, arithmetic and copies ran while one was open for 13% of the time, Pallas kernels for 1%

profile of v1, /device:TPU:2, one launch (start us, length us, event | category | flops | bytes accessed | tf_op | source)
XLA Modules:
  0.0 168.6 jit_solution(10758083431547445630)
XLA Ops:
  0.7 3.4 %dynamic-slice_bitcast_fusion.8 = (bf16[384,1024]{1,0:T(8,128)(2,1)S(1)}, bf16[384,1024]{1,0:T(8,128)(2,1)}, bf16[384,1024]{1,0:T(8,128)(2,1)}, bf16[384,1024]{1,0:T(8,128)(2,1)}) fusion(bf16[1,384,4096]{2,1,0:T(8,128)(2,1)} %param.19, s32[]{:T(128)S(6)} %select_n.88, s32[]{:T(128)S(6)} %select_n.81, s32[]{:T(128)S(6)} %select_n.79, s32[]{:T(128)S(6)} %select_n.83), kind=kLoop, calls=%fused_computation.38 | loop fusion | bytes 6291472 | tf_op jit(solution)/shard_map/dynamic_slice | solution.py:30
  4.1 1.6 collective-permute-start
  5.7 1.7 collective-permute-start.1
  7.4 2.0 %collective-permute-start.2 = (bf16[384,1024]{1,0:T(8,128)(2,1)}, bf16[384,1024]{1,0:T(8,128)(2,1)}, u32[]{:S(2)}, u32[]{:S(2)}) collective-permute-start(bf16[384,1024]{1,0:T(8,128)(2,1)} %get-tuple-element.27), channel_id=1, source_target_pairs={{0,2},{1,3},{2,0},{3,1},{4,6},{5,7},{6,4},{7,5},{8,10},{9,11},{10,... | collective-permute-start | bytes 2359304 | tf_op jit(solution)/shard_map/ppermute | solution.py:15
  10.0 0.2 fusion.44
  10.8 0.6 select_convert_fusion
  11.4 1.5 fusion
  12.9 12.2 %all-to-all-start = ((bf16[64,8,1024]{2,1,0:T(8,128)(2,1)}), bf16[64,8,1024]{2,1,0:T(8,128)(2,1)}, u32[]{:S(2)}, u32[]{:S(2)}) async-start(bf16[64,8,1024]{2,1,0:T(8,128)(2,1)} %fusion), calls=%async_computation | async-start | bytes 2097152 | tf_op jit(solution)/shard_map/all_to_all | solution.py:182
  25.1 3.5 %dynamic-slice_bitcast_fusion = (bf16[1024,384]{1,0:T(8,128)(2,1)S(1)}, bf16[1024,384]{1,0:T(8,128)(2,1)S(1)}, bf16[1024,384]{1,0:T(8,128)(2,1)S(1)}, bf16[1024,...) fusion(bf16[1,4096,384]{2,1,0:T(8,128)(2,1)} %param.18, ...), kind=kLoop, calls=%fused_computation.30 | loop fusion | bytes 12582928 | tf_op jit(solution)/shard_map/dynamic_slice | solution.py:30
  28.6 1.3 pad_maximum_fusion
  29.8 1.3 pad_maximum_fusion.1
  31.1 1.3 pad_maximum_fusion.2
  32.5 10.5 %collective-permute-done.2 = bf16[384,1024]{1,0:T(8,128)(2,1)} collective-permute-done((bf16[384,1024]{1,0:T(8,128)(2,1)}, bf16[384,1024]{1,0:T(8,128)(2,1)}, u32[]{:S(2)}, u32[]{:S(2)}) %collective-permute-start.2) | collective-permute-done | bytes 786464 | tf_op jit(solution)/shard_map/ppermute | solution.py:15
  43.0 1.3 copy.77.parents_ref
  44.4 2.0 %shard_map.165 = f32[32,32]{1,0:T(8,128)} custom-call(s32[32,1]{1,0:T(8,128)} %copy.77.parents_ref), custom_call_target="tpu_custom_call" | custom-call | flops 23069999104 | bytes 8192 | tf_op jit(solution)/shard_map/pallas_call | solution.py:75
  46.4 7.4 %all-to-all-done = bf16[64,8,1024]{2,1,0:T(8,128)(2,1)} async-done(((bf16[64,8,1024]{2,1,0:T(8,128)(2,1)}), bf16[64,8,1024]{2,1,0:T(8,128)(2,1)}, u32[]{:S(2)}, u32[]{:S(2)}) %all-to-all-start) | async-done | bytes 1048608 | tf_op jit(solution)/shard_map/all_to_all | solution.py:182
  53.8 0.7 collective-permute-start.3
  54.5 2.6 %collective-permute-start.4 = (bf16[512,1024]{1,0:T(8,128)(2,1)}, bf16[512,1024]{1,0:T(8,128)(2,1)S(1)}, u32[]{:S(2)}, u32[]{:S(2)}) collective-permute-start(bf16[512,1024]{1,0:T(8,128)(2,1)} %bitcast.19), channel_id=1, source_target_pairs={{0,3},{1,0},{2,1},{3,2},{4,7},{5,4},{6,5},{7,6},{8,11},{9,8},{10,9... | collective-permute-start | bytes 3145736 | tf_op jit(solution)/shard_map/ppermute | solution.py:15
  57.0 2.7 %fusion.55 = f32[512,768]{1,0:T(8,128)S(1)} fusion(bf16[1024,768]{1,0:T(8,128)(2,1)} %pad_maximum_fusion, bf16[64,8,1024]{2,1,0:T(8,128)(2,1)} %all-to-all-done), kind=kOutput, calls=%fused_computation.99 | convolution fusion | flops 805306368 | bytes 4194304 | tf_op jit(solution)/shard_map/dot_general | solution.py:41
  59.7 19.4 %collective-permute-done.3 = bf16[512,1024]{1,0:T(8,128)(2,1)S(1)} collective-permute-done((bf16[512,1024]{1,0:T(8,128)(2,1)}, bf16[512,1024]{1,0:T(8,128)(2,1)S(1)}, u32[]{:S(2)}, u32[]{:S(2)}) %collective-permute-start.3) | collective-permute-done | bytes 1048608 | tf_op jit(solution)/shard_map/ppermute | solution.py:15
  79.3 3.5 %collective-permute-start.6 = (bf16[256,1024]{1,0:T(8,128)(2,1)S(1)}, bf16[256,1024]{1,0:T(8,128)(2,1)S(1)}, u32[]{:S(2)}, u32[]{:S(2)}) collective-permute-start(bf16[256,1024]{1,0:T(8,128)(2,1)S(1)} %slice.33), channel_id=1, source_target_pairs={{0,3},{1,0},{2,1},{3,2},{4,7},{5,4},{6,5},{7,6},{8,11},{9,8},{10,9... | collective-permute-start | bytes 1572872 | tf_op jit(solution)/shard_map/ppermute | solution.py:15
  82.8 1.0 fusion.61
  83.8 1.0 fusion.62
  84.8 7.4 %collective-permute-done.5 = bf16[256,1024]{1,0:T(8,128)(2,1)S(1)} collective-permute-done((bf16[256,1024]{1,0:T(8,128)(2,1)S(1)}, bf16[256,1024]{1,0:T(8,128)(2,1)S(1)}, u32[]{:S(2)}, u32[]{:S(2)}) %collective-permute-start.5) | collective-permute-done | bytes 524320 | tf_op jit(solution)/shard_map/ppermute | solution.py:15
  92.2 1.0 add_add_fusion
  93.2 0.2 fusion.17
  93.5 3.3 %collective-permute-start.8 = (bf16[512,384]{1,0:T(8,128)(2,1)S(1)}, bf16[512,384]{1,0:T(8,128)(2,1)S(1)}, u32[]{:S(2)}, u32[]{:S(2)}) collective-permute-start(bf16[512,384]{1,0:T(8,128)(2,1)S(1)} %fusion.17), channel_id=1, source_target_pairs={{0,3},{1,0},{2,1},{3,2},{4,7},{5,4},{6,5},{7,6},{8,11},{9,8},{10,9... | collective-permute-start | bytes 1179656 | tf_op jit(solution)/shard_map/ppermute | solution.py:15
  96.8 0.7 fusion.63
  97.5 5.0 %collective-permute-done.8 = bf16[512,384]{1,0:T(8,128)(2,1)S(1)} collective-permute-done((bf16[512,384]{1,0:T(8,128)(2,1)S(1)}, bf16[512,384]{1,0:T(8,128)(2,1)S(1)}, u32[]{:S(2)}, u32[]{:S(2)}) %collective-permute-start.8) | collective-permute-done | bytes 393248 | tf_op jit(solution)/shard_map/ppermute | solution.py:15
  102.6 3.8 %collective-permute-start.10 = (bf16[256,384]{1,0:T(8,128)(2,1)S(1)}, bf16[256,384]{1,0:T(8,128)(2,1)S(1)}, u32[]{:S(2)}, u32[]{:S(2)}) collective-permute-start(bf16[256,384]{1,0:T(8,128)(2,1)S(1)} %slice.37), channel_id=1, source_target_pairs={{0,3},{1,0},{2,1},{3,2},{4,7},{5,4},{6,5},{7,6},{8,11},{9,8},{10,9... | collective-permute-start | bytes 589832 | tf_op jit(solution)/shard_map/ppermute | solution.py:15
  106.5 1.8 %fusion.64 = f32[512,1024]{1,0:T(8,128)S(1)} fusion(bf16[512,384]{1,0:T(8,128)(2,1)S(1)} %collective-permute-done.7, bf16[384,1024]{1,0:T(8,128)(2,1)} %collective-permute-done), kind=kOutput, calls=%fused_computation.108 | convolution fusion | flops 402653184 | bytes 3276800 | tf_op jit(solution)/shard_map/dot_general | solution.py:43
  108.4 1.8 %fusion.65 = f32[512,1024]{1,0:T(8,128)S(1)} fusion(bf16[512,384]{1,0:T(8,128)(2,1)S(1)} %collective-permute-done.8, bf16[384,1024]{1,0:T(8,128)(2,1)} %collective-permute-done.1), kind=kOutput, calls=%fused_computation.109 | convolution fusion | flops 402653184 | bytes 3276800 | tf_op jit(solution)/shard_map/dot_general | solution.py:43
  110.2 3.2 %collective-permute-done.9 = bf16[256,384]{1,0:T(8,128)(2,1)S(1)} collective-permute-done((bf16[256,384]{1,0:T(8,128)(2,1)S(1)}, bf16[256,384]{1,0:T(8,128)(2,1)S(1)}, u32[]{:S(2)}, u32[]{:S(2)}) %collective-permute-start.9) | collective-permute-done | bytes 196640 | tf_op jit(solution)/shard_map/ppermute | solution.py:15
  113.4 2.9 %fusion.8 = bf16[64,8,1024]{2,1,0:T(8,128)(2,1)} fusion(f32[512,1024]{1,0:T(8,128)S(1)} %fusion.65, f32[512,1024]{1,0:T(8,128)S(1)} %fusion.63, f32[512,1024]{1,0:T(8,128)S(1)} %fusion.64, bf16[384,1024]{1,0:T(8,128)(2,1)} %collective-permute-done.2, bf16[256,384]{1,0:T(8,128)(2,1)S(1)} %collective-permute-done.10, ...), kind=kOutput, calls=%fused_computation.21 | convolution fusion | flops 405536768 | bytes 8519680 | tf_op jit(solution)/shard_map/dot_general | solution.py:43
  116.3 9.3 %all-to-all-start.1 = ((bf16[64,8,1024]{2,1,0:T(8,128)(2,1)}), bf16[64,8,1024]{2,1,0:T(8,128)(2,1)S(1)}, u32[]{:S(2)}, u32[]{:S(2)}) async-start(bf16[64,8,1024]{2,1,0:T(8,128)(2,1)} %fusion.8), calls=%async_computation.1 | async-start | bytes 2097152 | tf_op jit(solution)/shard_map/all_to_all | solution.py:195
  126.3 0.3 fusion.59
  126.6 27.8 %all-to-all-done.1 = bf16[64,8,1024]{2,1,0:T(8,128)(2,1)S(1)} async-done(((bf16[64,8,1024]{2,1,0:T(8,128)(2,1)}), bf16[64,8,1024]{2,1,0:T(8,128)(2,1)S(1)}, u32[]{:S(2)}, u32[]{:S(2)}) %all-to-all-start.1) | async-done | bytes 1048608 | tf_op jit(solution)/shard_map/all_to_all | solution.py:195
  154.4 0.3 fusion.15
  154.7 0.7 broadcast_in_dim.78
  155.5 3.4 %all-to-all-start.2 = ((bf16[4,32,1024]{2,1,0:T(8,128)(2,1)}), bf16[4,32,1024]{2,1,0:T(8,128)(2,1)S(1)}, u32[]{:S(2)}, u32[]{:S(2)}) async-start(bf16[4,32,1024]{2,1,0:T(8,128)(2,1)} %broadcast_in_dim.78), calls=%async_computation.2 | async-start | bytes 524288 | tf_op jit(solution)/shard_map/all_to_all | solution.py:55
  159.0 6.5 %all-to-all-done.2 = bf16[4,32,1024]{2,1,0:T(8,128)(2,1)S(1)} async-done(((bf16[4,32,1024]{2,1,0:T(8,128)(2,1)}), bf16[4,32,1024]{2,1,0:T(8,128)(2,1)S(1)}, u32[]{:S(2)}, u32[]{:S(2)}) %all-to-all-start.2) | async-done | bytes 262176 | tf_op jit(solution)/shard_map/all_to_all | solution.py:55
  165.8 0.3 convolution_convert_fusion.2
  166.2 0.3 fusion.60
  166.6 0.3 fusion.25
  166.9 0.3 convolution_convert_fusion.1
  167.3 0.3 convolution_bitcast_fusion
  167.6 0.3 fusion.7
  167.9 0.7 copy.102
  (76 shorter events, 2.3 us)
Async XLA Ops:
  0.6 165.2 %copy-start = (bf16[4096,128]{1,0:T(8,128)(2,1)S(1)}, bf16[4096,128]{1,0:T(8,128)(2,1)}, u32[]{:S(2)}) copy-start(bf16[4096,128]{1,0:T(8,128)(2,1)} %param.21) | copy-start | bytes 3145732
  0.7 8.7 %copy-start.12 = (f32[32,8]{0,1:T(8,128)S(1)}, f32[32,8]{0,1:T(8,128)}, u32[]{:S(2)}) copy-start(f32[32,8]{0,1:T(8,128)} %param.16) | copy-start | bytes 3076
  0.7 8.8 %copy-start.14 = (s32[32,8]{0,1:T(8,128)S(1)}, s32[32,8]{0,1:T(8,128)}, u32[]{:S(2)}) copy-start(s32[32,8]{0,1:T(8,128)} %param.15) | copy-start | bytes 3076
  4.1 7.3 %copy-start.5 = (bf16[32,1024]{1,0:T(8,128)(2,1)S(1)}, bf16[32,1024]{1,0:T(8,128)(2,1)}, u32[]{:S(2)}) copy-start(bf16[32,1024]{1,0:T(8,128)(2,1)} %param.14) | copy-start | bytes 196612
  4.1 28.4 %collective-permute-start = (bf16[384,1024]{1,0:T(8,128)(2,1)}, bf16[384,1024]{1,0:T(8,128)(2,1)}, u32[]{:S(2)}, u32[]{:S(2)}) collective-permute-start(bf16[384,1024]{1,0:T(8,128)(2,1)} %get-tuple-element.25), channel_id=1, source_target_pairs={{0,1},{1,2},{2,3},{3,0},{4,5},{5,6},{6,7},{7,4},{8,9},{9,10},{10,1... | collective-permute-start | bytes 2359304 | tf_op jit(solution)/shard_map/ppermute | solution.py:15
  5.7 26.8 %collective-permute-start.1 = (bf16[384,1024]{1,0:T(8,128)(2,1)}, bf16[384,1024]{1,0:T(8,128)(2,1)}, u32[]{:S(2)}, u32[]{:S(2)}) collective-permute-start(bf16[384,1024]{1,0:T(8,128)(2,1)} %get-tuple-element.26), channel_id=1, source_target_pairs={{0,3},{1,0},{2,1},{3,2},{4,7},{5,4},{6,5},{7,6},{8,11},{9,8},{10,9... | collective-permute-start | bytes 2359304 | tf_op jit(solution)/shard_map/ppermute | solution.py:15
  7.4 35.7 %collective-permute-start.2 = (bf16[384,1024]{1,0:T(8,128)(2,1)}, bf16[384,1024]{1,0:T(8,128)(2,1)}, u32[]{:S(2)}, u32[]{:S(2)}) collective-permute-start(bf16[384,1024]{1,0:T(8,128)(2,1)} %get-tuple-element.27), channel_id=1, source_target_pairs={{0,2},{1,3},{2,0},{3,1},{4,6},{5,7},{6,4},{7,5},{8,10},{9,11},{10,... | collective-permute-start | bytes 2359304 | tf_op jit(solution)/shard_map/ppermute | solution.py:15
  12.9 40.9 %all-to-all-start = ((bf16[64,8,1024]{2,1,0:T(8,128)(2,1)}), bf16[64,8,1024]{2,1,0:T(8,128)(2,1)}, u32[]{:S(2)}, u32[]{:S(2)}) async-start(bf16[64,8,1024]{2,1,0:T(8,128)(2,1)} %fusion), calls=%async_computation | async-start | bytes 2097152 | tf_op jit(solution)/shard_map/all_to_all | solution.py:182
  53.8 25.3 %collective-permute-start.3 = (bf16[512,1024]{1,0:T(8,128)(2,1)}, bf16[512,1024]{1,0:T(8,128)(2,1)S(1)}, u32[]{:S(2)}, u32[]{:S(2)}) collective-permute-start(bf16[512,1024]{1,0:T(8,128)(2,1)} %bitcast.19), channel_id=1, source_target_pairs={{0,1},{1,2},{2,3},{3,0},{4,5},{5,6},{6,7},{7,4},{8,9},{9,10},{10,1... | collective-permute-start | bytes 3145736 | tf_op jit(solution)/shard_map/ppermute | solution.py:15
  54.5 24.8 %collective-permute-start.4 = (bf16[512,1024]{1,0:T(8,128)(2,1)}, bf16[512,1024]{1,0:T(8,128)(2,1)S(1)}, u32[]{:S(2)}, u32[]{:S(2)}) collective-permute-start(bf16[512,1024]{1,0:T(8,128)(2,1)} %bitcast.19), channel_id=1, source_target_pairs={{0,3},{1,0},{2,1},{3,2},{4,7},{5,4},{6,5},{7,6},{8,11},{9,8},{10,9... | collective-permute-start | bytes 3145736 | tf_op jit(solution)/shard_map/ppermute | solution.py:15
  59.7 23.1 %copy-start.1 = (bf16[1024,768]{1,0:T(8,128)(2,1)S(1)}, bf16[1024,768]{1,0:T(8,128)(2,1)}, u32[]{:S(2)}) copy-start(bf16[1024,768]{1,0:T(8,128)(2,1)} %pad_maximum_fusion.1) | copy-start | bytes 4718596
  79.2 13.0 %collective-permute-start.5 = (bf16[256,1024]{1,0:T(8,128)(2,1)S(1)}, bf16[256,1024]{1,0:T(8,128)(2,1)S(1)}, u32[]{:S(2)}, u32[]{:S(2)}) collective-permute-start(bf16[256,1024]{1,0:T(8,128)(2,1)S(1)} %slice.32), channel_id=1, source_target_pairs={{0,1},{1,2},{2,3},{3,0},{4,5},{5,6},{6,7},{7,4},{8,9},{9,10},{10,1... | collective-permute-start | bytes 1572872 | tf_op jit(solution)/shard_map/ppermute | solution.py:15
  79.3 4.5 %copy-start.2 = (bf16[1024,768]{1,0:T(8,128)(2,1)S(1)}, bf16[1024,768]{1,0:T(8,128)(2,1)}, u32[]{:S(2)}) copy-start(bf16[1024,768]{1,0:T(8,128)(2,1)} %pad_maximum_fusion.2) | copy-start | bytes 4718596
  79.3 12.9 %collective-permute-start.6 = (bf16[256,1024]{1,0:T(8,128)(2,1)S(1)}, bf16[256,1024]{1,0:T(8,128)(2,1)S(1)}, u32[]{:S(2)}, u32[]{:S(2)}) collective-permute-start(bf16[256,1024]{1,0:T(8,128)(2,1)S(1)} %slice.33), channel_id=1, source_target_pairs={{0,3},{1,0},{2,1},{3,2},{4,7},{5,4},{6,5},{7,6},{8,11},{9,8},{10,9... | collective-permute-start | bytes 1572872 | tf_op jit(solution)/shard_map/ppermute | solution.py:15
  93.5 9.1 %collective-permute-start.8 = (bf16[512,384]{1,0:T(8,128)(2,1)S(1)}, bf16[512,384]{1,0:T(8,128)(2,1)S(1)}, u32[]{:S(2)}, u32[]{:S(2)}) collective-permute-start(bf16[512,384]{1,0:T(8,128)(2,1)S(1)} %fusion.17), channel_id=1, source_target_pairs={{0,3},{1,0},{2,1},{3,2},{4,7},{5,4},{6,5},{7,6},{8,11},{9,8},{10,9... | collective-permute-start | bytes 1179656 | tf_op jit(solution)/shard_map/ppermute | solution.py:15
  96.8 9.6 %collective-permute-start.7 = (bf16[512,384]{1,0:T(8,128)(2,1)S(1)}, bf16[512,384]{1,0:T(8,128)(2,1)S(1)}, u32[]{:S(2)}, u32[]{:S(2)}) collective-permute-start(bf16[512,384]{1,0:T(8,128)(2,1)S(1)} %fusion.17), channel_id=1, source_target_pairs={{0,1},{1,2},{2,3},{3,0},{4,5},{5,6},{6,7},{7,4},{8,9},{9,10},{10,1... | collective-permute-start | bytes 1179656 | tf_op jit(solution)/shard_map/ppermute | solution.py:15
  102.6 7.7 %collective-permute-start.10 = (bf16[256,384]{1,0:T(8,128)(2,1)S(1)}, bf16[256,384]{1,0:T(8,128)(2,1)S(1)}, u32[]{:S(2)}, u32[]{:S(2)}) collective-permute-start(bf16[256,384]{1,0:T(8,128)(2,1)S(1)} %slice.37), channel_id=1, source_target_pairs={{0,3},{1,0},{2,1},{3,2},{4,7},{5,4},{6,5},{7,6},{8,11},{9,8},{10,9... | collective-permute-start | bytes 589832 | tf_op jit(solution)/shard_map/ppermute | solution.py:15
  106.4 7.0 %collective-permute-start.9 = (bf16[256,384]{1,0:T(8,128)(2,1)S(1)}, bf16[256,384]{1,0:T(8,128)(2,1)S(1)}, u32[]{:S(2)}, u32[]{:S(2)}) collective-permute-start(bf16[256,384]{1,0:T(8,128)(2,1)S(1)} %slice.36), channel_id=1, source_target_pairs={{0,1},{1,2},{2,3},{3,0},{4,5},{5,6},{6,7},{7,4},{8,9},{9,10},{10,1... | collective-permute-start | bytes 589832 | tf_op jit(solution)/shard_map/ppermute | solution.py:15
  116.3 10.0 %copy-start.4 = (bf16[32,2048]{1,0:T(8,128)(2,1)S(1)}, bf16[32,2048]{1,0:T(8,128)(2,1)}, u32[]{:S(2)}) copy-start(bf16[32,2048]{1,0:T(8,128)(2,1)} %param.23) | copy-start | bytes 393220
  116.3 10.0 %copy-start.10 = (bf16[1,128,128]{2,1,0:T(8,128)(2,1)S(1)}, bf16[1,128,128]{2,1,0:T(8,128)(2,1)}, u32[]{:S(2)}) copy-start(bf16[1,128,128]{2,1,0:T(8,128)(2,1)} %param.24) | copy-start | bytes 98308
  116.3 38.1 %copy-start.7 = (bf16[512,32]{0,1:T(8,128)(2,1)S(1)}, bf16[512,32]{0,1:T(8,128)(2,1)}, u32[]{:S(2)}) copy-start(bf16[512,32]{0,1:T(8,128)(2,1)} %get-tuple-element.42) | copy-start | bytes 98308
  116.3 38.1 %all-to-all-start.1 = ((bf16[64,8,1024]{2,1,0:T(8,128)(2,1)}), bf16[64,8,1024]{2,1,0:T(8,128)(2,1)S(1)}, u32[]{:S(2)}, u32[]{:S(2)}) async-start(bf16[64,8,1024]{2,1,0:T(8,128)(2,1)} %fusion.8), calls=%async_computation.1 | async-start | bytes 2097152 | tf_op jit(solution)/shard_map/all_to_all | solution.py:195
  126.2 32.6 %copy-start.11 = (f32[32,32]{1,0:T(8,128)S(1)}, f32[32,32]{1,0:T(8,128)}, u32[]{:S(2)}) copy-start(f32[32,32]{1,0:T(8,128)} %shard_map.165) | copy-start | bytes 12292
  154.7 11.5 %copy-start.6 = (bf16[32,1024]{1,0:T(8,128)(2,1)}, bf16[32,1024]{1,0:T(8,128)(2,1)S(1)}, u32[]{:S(2)}) copy-start(bf16[32,1024]{1,0:T(8,128)(2,1)S(1)} %fusion.30) | copy-start | bytes 196612
  154.7 11.1 %copy-start.8 = (f32[4096]{0:T(1024)S(1)}, f32[4096]{0:T(1024)}, u32[]{:S(2)}) copy-start(f32[4096]{0:T(1024)} %param.20) | copy-start | bytes 49156
  155.5 10.1 %all-to-all-start.2 = ((bf16[4,32,1024]{2,1,0:T(8,128)(2,1)}), bf16[4,32,1024]{2,1,0:T(8,128)(2,1)S(1)}, u32[]{:S(2)}, u32[]{:S(2)}) async-start(bf16[4,32,1024]{2,1,0:T(8,128)(2,1)} %broadcast_in_dim.78), calls=%async_computation.2 | async-start | bytes 524288 | tf_op jit(solution)/shard_map/all_to_all | solution.py:55
  165.6 1.3 copy-start.3
  166.2 1.4 copy-start.9
  166.2 1.1 copy-start.15
  167.2 1.4 copy-start.13

commit v2 on v1

--- a/solution.py
+++ b/solution.py
@@ -17,9 +17,12 @@
 
 def gathered_ring(rows):
     half = rows.shape[0] // 2
-    before = shifted(rows, 1)
-    after = shifted(rows, -1)
-    opposite = jnp.concatenate([shifted(before[:half], 1), shifted(after[half:], -1)], axis=0)
+    upper, lower = rows[:half], rows[half:]
+    before_upper, after_lower = shifted(upper, 1), shifted(lower, -1)
+    before_lower, after_upper = shifted(lower, 1), shifted(upper, -1)
+    opposite = jnp.concatenate([shifted(before_upper, 1), shifted(after_lower, -1)], axis=0)
+    before = jnp.concatenate([before_upper, before_lower], axis=0)
+    after = jnp.concatenate([after_upper, after_lower], axis=0)
     return rows, before, after, opposite
 
 
@@ -171,18 +174,19 @@
     ).astype(jnp.bfloat16)
     outgoing = outgoing.reshape(expert_count, capacity, column_count)
     down_received = sent_around(down_sent)
-    down_received, parents = lax.optimization_barrier((down_received, parents))
+    down_whole = jnp.concatenate([down_own, *down_received], axis=0)
+    down_whole, parents = lax.optimization_barrier((down_whole, parents))
     related = ancestry(parents)
-    down_blocks = [down_own, *down_received]
     hidden_units = w_gate.shape[2]
     both_weights = [
         jnp.concatenate(pair, axis=1)
         for pair in zip(around(w_gate[0], 0, column_count), around(w_up[0], 0, column_count))
     ]
     received = lax.all_to_all(outgoing, "dp", split_axis=0, concat_axis=0, tiled=True)
-    received, down_blocks, both_weights, related = lax.optimization_barrier(
-        (received, down_blocks, both_weights, related)
-    )
+    received, down_whole, both_weights, related = lax.optimization_barrier(
+        (received, down_whole, both_weights, related)
+    )
+    down_blocks = jnp.split(down_whole, lax.axis_size("tp"))
     chunk = capacity // CHUNKS
     returned = []
     for part in range(CHUNKS):

time: 169 us -> 166 us (0.982)
  waiting for transfers between devices: 87.3 us -> 80 us
  starting transfers between devices: 44.1 us -> 48.1 us
  matrix products: 16.7 us -> 12.8 us
  other arithmetic: 5.75 us -> 8.9 us
    ppermute x11 -> x15, waiting for transfers between devices: 45.6 us -> 41.3 us  [shifted(): lax.ppermute(value, 'tp', [(i, (i + step) % size) for i in range(size)])]
    ppermute x11 -> x15, starting transfers between devices: 19.2 us -> 23.3 us  [shifted(): lax.ppermute(value, 'tp', [(i, (i + step) % size) for i in range(size)])]
    dot_general x6, matrix products: 9.52 us -> 6.14 us  [summed_products(): total = total + jnp.dot(block, weight, preferred_element_type=jnp.float32)]
    all_to_all x1, waiting for transfers between devices: 7.43 us -> 4.33 us  [on_device(): lax.all_to_all(outgoing, 'dp', split_axis=0, concat_axis=0, tiled=True)]
    concatenate x0 -> x1, other arithmetic: none -> 3.08 us  [on_device(): down_whole = jnp.concatenate([down_own, *down_received], axis=0)]
  transfers between devices with their start and end apart: 14 -> 18, of which waited for: 9 -> 10; matrix products, arithmetic and copies ran while one was open for 13% -> 13% of each run, Pallas kernels for 1% -> 1%
where the time goes in v2:
time: 166 us
  waiting for transfers between devices  80 us (48%)
  starting transfers between devices  48.1 us (29%)
  matrix products  12.8 us (8%)
  local copies, waits for them, and re-layouts  12.2 us (7%)
  other arithmetic  8.9 us (5%)
  Pallas kernels  1.98 us (1%)
  between operations  1.8 us (1%)
    ppermute x15, waiting for transfers between devices, shifted(): lax.ppermute(value, 'tp', [(i, (i + step) % size) for i in range(size)])  41.3 us
    all_to_all x1, waiting for transfers between devices, on_device(): lax.all_to_all(made.reshape(expert_count, chunk, column_count), 'dp', spl...  27.8 us
    ppermute x15, starting transfers between devices, shifted(): lax.ppermute(value, 'tp', [(i, (i + step) % size) for i in range(size)])  23.3 us
    all_to_all x1, starting transfers between devices, on_device(): lax.all_to_all(outgoing, 'dp', split_axis=0, concat_axis=0, tiled=True)  12.2 us
    all_to_all x1, starting transfers between devices, on_device(): lax.all_to_all(made.reshape(expert_count, chunk, column_count), 'dp', spl...  7.92 us
    dynamic_slice x2, local copies, waits for them, and re-layouts, around(): lax.dynamic_slice_in_dim(value, (index + step) % count * size, size, dim)  6.85 us
    all_to_all x1, waiting for transfers between devices, copy_for_each(): return lax.all_to_all(copies, axis, split_axis=0, concat_axis=0, tiled=True)  6.58 us
    dot_general x6, matrix products, summed_products(): total = total + jnp.dot(block, weight, preferred_element_type=jnp.float32)  6.14 us
  transfers between devices with their start and end apart: 18, of which 10 were waited for; matrix products, arithmetic and copies ran while one was open for 13% of the time, Pallas kernels for 1%

profile of v2, /device:TPU:2, one launch (start us, length us, event | category | flops | bytes accessed | tf_op | source)
XLA Modules:
  0.0 165.7 jit_solution(1566047562915496127)
XLA Ops:
  0.7 3.4 %dynamic-slice_bitcast_fusion.8 = (bf16[384,1024]{1,0:T(8,128)(2,1)S(1)}, bf16[384,1024]{1,0:T(8,128)(2,1)}, bf16[384,1024]{1,0:T(8,128)(2,1)}, bf16[384,1024]{1,0:T(8,128)(2,1)}) fusion(bf16[1,384,4096]{2,1,0:T(8,128)(2,1)} %param.19, s32[]{:T(128)S(6)} %select_n.88, s32[]{:T(128)S(6)} %select_n.81, s32[]{:T(128)S(6)} %select_n.79, s32[]{:T(128)S(6)} %select_n.83), kind=kLoop, calls=%fused_computation.55 | loop fusion | bytes 6291472 | tf_op jit(solution)/shard_map/dynamic_slice | solution.py:33
  4.1 1.6 collective-permute-start
  5.7 1.7 %collective-permute-start.1 = (bf16[384,1024]{1,0:T(8,128)(2,1)}, bf16[384,1024]{1,0:T(8,128)(2,1)}, u32[]{:S(2)}, u32[]{:S(2)}) collective-permute-start(bf16[384,1024]{1,0:T(8,128)(2,1)} %get-tuple-element.21), channel_id=1, source_target_pairs={{0,3},{1,0},{2,1},{3,2},{4,7},{5,4},{6,5},{7,6},{8,11},{9,8},{10,9... | collective-permute-start | bytes 2359304 | tf_op jit(solution)/shard_map/ppermute | solution.py:15
  7.4 2.0 %collective-permute-start.2 = (bf16[384,1024]{1,0:T(8,128)(2,1)}, bf16[384,1024]{1,0:T(8,128)(2,1)}, u32[]{:S(2)}, u32[]{:S(2)}) collective-permute-start(bf16[384,1024]{1,0:T(8,128)(2,1)} %get-tuple-element.22), channel_id=1, source_target_pairs={{0,2},{1,3},{2,0},{3,1},{4,6},{5,7},{6,4},{7,5},{8,10},{9,11},{10,... | collective-permute-start | bytes 2359304 | tf_op jit(solution)/shard_map/ppermute | solution.py:15
  10.7 0.6 select_convert_fusion
  11.4 1.4 fusion
  12.8 12.2 %all-to-all-start = ((bf16[64,8,1024]{2,1,0:T(8,128)(2,1)}), bf16[64,8,1024]{2,1,0:T(8,128)(2,1)}, u32[]{:S(2)}, u32[]{:S(2)}) async-start(bf16[64,8,1024]{2,1,0:T(8,128)(2,1)} %fusion), calls=%async_computation | async-start | bytes 2097152 | tf_op jit(solution)/shard_map/all_to_all | solution.py:185
  25.1 3.5 %dynamic-slice_bitcast_fusion = (bf16[1024,384]{1,0:T(8,128)(2,1)S(1)}, bf16[1024,384]{1,0:T(8,128)(2,1)S(1)}, bf16[1024,384]{1,0:T(8,128)(2,1)S(1)}, bf16[1024,...) fusion(bf16[1,4096,384]{2,1,0:T(8,128)(2,1)} %param.18, ...), kind=kLoop, calls=%fused_computation.47 | loop fusion | bytes 12582928 | tf_op jit(solution)/shard_map/dynamic_slice | solution.py:33
  28.7 1.3 pad_maximum_fusion.2
  29.9 1.3 pad_maximum_fusion.1
  31.2 1.3 pad_maximum_fusion.3
  32.6 10.5 %collective-permute-done.2 = bf16[384,1024]{1,0:T(8,128)(2,1)} collective-permute-done((bf16[384,1024]{1,0:T(8,128)(2,1)}, bf16[384,1024]{1,0:T(8,128)(2,1)}, u32[]{:S(2)}, u32[]{:S(2)}) %collective-permute-start.2) | collective-permute-done | bytes 786464 | tf_op jit(solution)/shard_map/ppermute | solution.py:15
  43.0 3.1 %pad_maximum_fusion = bf16[1536,1024]{1,0:T(8,128)(2,1)} fusion(bf16[384,1024]{1,0:T(8,128)(2,1)} %collective-permute-done.2, bf16[384,1024]{1,0:T(8,128)(2,1)} %collective-permute-done.1, bf16[384,1024]{1,0:T(8,128)(2,1)} %collective-permute-done, bf16[384,1024]{1,0:T(8,128)(2,1)S(1)} %get-tuple-element.42), kind=kLoop, calls=%fused_computation | loop fusion | flops 12582912 | bytes 6291456 | tf_op jit(solution)/shard_map/concatenate | solution.py:177
  46.1 1.3 copy.77.parents_ref
  47.4 2.0 %shard_map.165 = f32[32,32]{1,0:T(8,128)} custom-call(s32[32,1]{1,0:T(8,128)} %copy.77.parents_ref), custom_call_target="tpu_custom_call" | custom-call | flops 23069999104 | bytes 8192 | tf_op jit(solution)/shard_map/pallas_call | solution.py:78
  49.4 4.3 %all-to-all-done = bf16[64,8,1024]{2,1,0:T(8,128)(2,1)} async-done(((bf16[64,8,1024]{2,1,0:T(8,128)(2,1)}), bf16[64,8,1024]{2,1,0:T(8,128)(2,1)}, u32[]{:S(2)}, u32[]{:S(2)}) %all-to-all-start) | async-done | bytes 1048608 | tf_op jit(solution)/shard_map/all_to_all | solution.py:185
  53.8 1.4 slice_bitcast_fusion.1
  55.2 0.8 collective-permute-start.3
  55.9 2.6 %collective-permute-start.6 = (bf16[256,1024]{1,0:T(8,128)(2,1)S(1)}, bf16[256,1024]{1,0:T(8,128)(2,1)S(1)}, u32[]{:S(2)}, u32[]{:S(2)}) collective-permute-start(bf16[256,1024]{1,0:T(8,128)(2,1)S(1)} %get-tuple-element.47), channel_id=1, source_target_pairs={{0,3},{1,0},{2,1},{3,2},{4,7},{5,4},{6,5},{7,6},{8,11},{9,8},{10,9... | collective-permute-start | bytes 1572872 | tf_op jit(solution)/shard_map/ppermute | solution.py:15
  58.5 2.0 %collective-permute-start.4 = (bf16[256,1024]{1,0:T(8,128)(2,1)S(1)}, bf16[256,1024]{1,0:T(8,128)(2,1)S(1)}, u32[]{:S(2)}, u32[]{:S(2)}) collective-permute-start(bf16[256,1024]{1,0:T(8,128)(2,1)S(1)} %get-tuple-element.47), channel_id=1, source_target_pairs={{0,1},{1,2},{2,3},{3,0},{4,5},{5,6},{6,7},{7,4},{8,9},{9,10},{10,1... | collective-permute-start | bytes 1572872 | tf_op jit(solution)/shard_map/ppermute | solution.py:15
  60.5 2.2 %fusion.22 = f32[512,768]{1,0:T(8,128)S(1)} fusion(bf16[1024,768]{1,0:T(8,128)(2,1)S(1)} %copy-done.4, bf16[64,8,1024]{2,1,0:T(8,128)(2,1)} %all-to-all-done), kind=kOutput, calls=%fused_computation.36 | convolution fusion | flops 805306368 | bytes 4194304 | tf_op jit(solution)/shard_map/dot_general | solution.py:44
  62.7 8.6 %collective-permute-done.3 = bf16[256,1024]{1,0:T(8,128)(2,1)S(1)} collective-permute-done((bf16[256,1024]{1,0:T(8,128)(2,1)S(1)}, bf16[256,1024]{1,0:T(8,128)(2,1)S(1)}, u32[]{:S(2)}, u32[]{:S(2)}) %collective-permute-start.3) | collective-permute-done | bytes 524320 | tf_op jit(solution)/shard_map/ppermute | solution.py:15
  71.3 3.2 %collective-permute-start.8 = (bf16[256,1024]{1,0:T(8,128)(2,1)S(1)}, bf16[256,1024]{1,0:T(8,128)(2,1)S(1)}, u32[]{:S(2)}, u32[]{:S(2)}) collective-permute-start(bf16[256,1024]{1,0:T(8,128)(2,1)S(1)} %collective-permute-done.6), channel_id=1, source_target_pairs={{0,3},{1,0},{2,1},{3,2},{4,7},{5,4},{6,5},{7,6},{8,11},{9,8},{10,9... | collective-permute-start | bytes 1572872 | tf_op jit(solution)/shard_map/ppermute | solution.py:15
  74.6 7.5 %collective-permute-done.5 = bf16[256,1024]{1,0:T(8,128)(2,1)S(1)} collective-permute-done((bf16[256,1024]{1,0:T(8,128)(2,1)S(1)}, bf16[256,1024]{1,0:T(8,128)(2,1)S(1)}, u32[]{:S(2)}, u32[]{:S(2)}) %collective-permute-start.5) | collective-permute-done | bytes 524320 | tf_op jit(solution)/shard_map/ppermute | solution.py:15
  82.1 1.0 fusion.13
  83.1 1.0 fusion.9
  84.1 7.5 %collective-permute-done.7 = bf16[256,1024]{1,0:T(8,128)(2,1)S(1)} collective-permute-done((bf16[256,1024]{1,0:T(8,128)(2,1)S(1)}, bf16[256,1024]{1,0:T(8,128)(2,1)S(1)}, u32[]{:S(2)}, u32[]{:S(2)}) %collective-permute-start.7) | collective-permute-done | bytes 524320 | tf_op jit(solution)/shard_map/ppermute | solution.py:15
  91.6 1.0 add_add_fusion
  92.9 3.0 %collective-permute-start.11 = (bf16[256,384]{1,0:T(8,128)(2,1)S(1)}, bf16[256,384]{1,0:T(8,128)(2,1)S(1)}, u32[]{:S(2)}, u32[]{:S(2)}) collective-permute-start(bf16[256,384]{1,0:T(8,128)(2,1)S(1)} %get-tuple-element.48), channel_id=1, source_target_pairs={{0,3},{1,0},{2,1},{3,2},{4,7},{5,4},{6,5},{7,6},{8,11},{9,8},{10,9... | collective-permute-start | bytes 589832 | tf_op jit(solution)/shard_map/ppermute | solution.py:15
  95.9 3.2 %collective-permute-start.12 = (bf16[256,384]{1,0:T(8,128)(2,1)S(1)}, bf16[256,384]{1,0:T(8,128)(2,1)S(1)}, u32[]{:S(2)}, u32[]{:S(2)}) collective-permute-start(bf16[256,384]{1,0:T(8,128)(2,1)S(1)} %get-tuple-element.49), channel_id=1, source_target_pairs={{0,3},{1,0},{2,1},{3,2},{4,7},{5,4},{6,5},{7,6},{8,11},{9,8},{10,9... | collective-permute-start | bytes 589832 | tf_op jit(solution)/shard_map/ppermute | solution.py:15
  99.2 0.7 fusion.30
  99.9 5.0 %collective-permute-done.9 = bf16[256,384]{1,0:T(8,128)(2,1)S(1)} collective-permute-done((bf16[256,384]{1,0:T(8,128)(2,1)S(1)}, bf16[256,384]{1,0:T(8,128)(2,1)S(1)}, u32[]{:S(2)}, u32[]{:S(2)}) %collective-permute-start.9) | collective-permute-done | bytes 196640 | tf_op jit(solution)/shard_map/ppermute | solution.py:15
  104.9 3.2 %collective-permute-start.14 = (bf16[256,384]{1,0:T(8,128)(2,1)S(1)}, bf16[256,384]{1,0:T(8,128)(2,1)S(1)}, u32[]{:S(2)}, u32[]{:S(2)}) collective-permute-start(bf16[256,384]{1,0:T(8,128)(2,1)S(1)} %collective-permute-done.12), channel_id=1, source_target_pairs={{0,3},{1,0},{2,1},{3,2},{4,7},{5,4},{6,5},{7,6},{8,11},{9,8},{10,9... | collective-permute-start | bytes 589832 | tf_op jit(solution)/shard_map/ppermute | solution.py:15
  108.2 0.7 fusion.28
  108.9 0.7 fusion.26
  109.7 2.1 %collective-permute-done.13 = bf16[256,384]{1,0:T(8,128)(2,1)S(1)} collective-permute-done((bf16[256,384]{1,0:T(8,128)(2,1)S(1)}, bf16[256,384]{1,0:T(8,128)(2,1)S(1)}, u32[]{:S(2)}, u32[]{:S(2)}) %collective-permute-start.13) | collective-permute-done | bytes 196640 | tf_op jit(solution)/shard_map/ppermute | solution.py:15
  111.8 1.7 %fusion.1 = bf16[64,8,1024]{2,1,0:T(8,128)(2,1)} fusion(f32[512,1024]{1,0:T(8,128)S(1)} %fusion.26, f32[512,1024]{1,0:T(8,128)S(1)} %fusion.30, f32[512,1024]{1,0:T(8,128)S(1)} %fusion.28, bf16[1536,1024]{1,0:T(8,128)(2,1)S(1)} %copy-done.1, bf16[256,384]{1,0:T(8,128)(2,1)S(1)} %collective-permute-done.14, bf16[256,384]{1,0:T(8,128)(2,1)S(1)} %collective-permute-done.13), kind=kOutput, calls=%fused_computation.9 | convolution fusion | flops 405536768 | bytes 8519680 | tf_op jit(solution)/shard_map/dot_general | solution.py:46
  113.5 7.9 %all-to-all-start.1 = ((bf16[64,8,1024]{2,1,0:T(8,128)(2,1)}), bf16[64,8,1024]{2,1,0:T(8,128)(2,1)S(1)}, u32[]{:S(2)}, u32[]{:S(2)}) async-start(bf16[64,8,1024]{2,1,0:T(8,128)(2,1)} %fusion.1), calls=%async_computation.1 | async-start | bytes 2097152 | tf_op jit(solution)/shard_map/all_to_all | solution.py:199
  122.2 0.3 fusion.79
  122.5 27.8 %all-to-all-done.1 = bf16[64,8,1024]{2,1,0:T(8,128)(2,1)S(1)} async-done(((bf16[64,8,1024]{2,1,0:T(8,128)(2,1)}), bf16[64,8,1024]{2,1,0:T(8,128)(2,1)S(1)}, u32[]{:S(2)}, u32[]{:S(2)}) %all-to-all-start.1) | async-done | bytes 1048608 | tf_op jit(solution)/shard_map/all_to_all | solution.py:199
  150.6 0.7 broadcast_in_dim.78
  151.3 4.6 %all-to-all-start.2 = ((bf16[4,32,1024]{2,1,0:T(8,128)(2,1)}), bf16[4,32,1024]{2,1,0:T(8,128)(2,1)S(1)}, u32[]{:S(2)}, u32[]{:S(2)}) async-start(bf16[4,32,1024]{2,1,0:T(8,128)(2,1)} %broadcast_in_dim.78), calls=%async_computation.2 | async-start | bytes 524288 | tf_op jit(solution)/shard_map/all_to_all | solution.py:58
  156.1 6.6 %all-to-all-done.2 = bf16[4,32,1024]{2,1,0:T(8,128)(2,1)S(1)} async-done(((bf16[4,32,1024]{2,1,0:T(8,128)(2,1)}), bf16[4,32,1024]{2,1,0:T(8,128)(2,1)S(1)}, u32[]{:S(2)}, u32[]{:S(2)}) %all-to-all-start.2) | async-done | bytes 262176 | tf_op jit(solution)/shard_map/all_to_all | solution.py:58
  163.0 0.3 convolution_convert_fusion.1
  163.3 0.3 convolution_convert_fusion.2
  163.7 0.3 fusion.80
  164.4 0.3 convolution_bitcast_fusion
  165.0 0.7 copy.102
  (87 shorter events, 3.3 us)
Async XLA Ops:
  0.6 162.3 %copy-start = (bf16[4096,128]{1,0:T(8,128)(2,1)S(1)}, bf16[4096,128]{1,0:T(8,128)(2,1)}, u32[]{:S(2)}) copy-start(bf16[4096,128]{1,0:T(8,128)(2,1)} %param.22) | copy-start | bytes 3145732
  0.7 8.8 %copy-start.14 = (f32[32,8]{0,1:T(8,128)S(1)}, f32[32,8]{0,1:T(8,128)}, u32[]{:S(2)}) copy-start(f32[32,8]{0,1:T(8,128)} %param.16) | copy-start | bytes 3076
  0.7 8.9 %copy-start.16 = (s32[32,8]{0,1:T(8,128)S(1)}, s32[32,8]{0,1:T(8,128)}, u32[]{:S(2)}) copy-start(s32[32,8]{0,1:T(8,128)} %param.15) | copy-start | bytes 3076
  0.7 10.7 %copy-start.7 = (bf16[32,1024]{1,0:T(8,128)(2,1)S(1)}, bf16[32,1024]{1,0:T(8,128)(2,1)}, u32[]{:S(2)}) copy-start(bf16[32,1024]{1,0:T(8,128)(2,1)} %param.14) | copy-start | bytes 196612
  4.1 28.4 %collective-permute-start = (bf16[384,1024]{1,0:T(8,128)(2,1)}, bf16[384,1024]{1,0:T(8,128)(2,1)}, u32[]{:S(2)}, u32[]{:S(2)}) collective-permute-start(bf16[384,1024]{1,0:T(8,128)(2,1)} %get-tuple-element.20), channel_id=1, source_target_pairs={{0,1},{1,2},{2,3},{3,0},{4,5},{5,6},{6,7},{7,4},{8,9},{9,10},{10,1... | collective-permute-start | bytes 2359304 | tf_op jit(solution)/shard_map/ppermute | solution.py:15
  5.7 26.8 %collective-permute-start.1 = (bf16[384,1024]{1,0:T(8,128)(2,1)}, bf16[384,1024]{1,0:T(8,128)(2,1)}, u32[]{:S(2)}, u32[]{:S(2)}) collective-permute-start(bf16[384,1024]{1,0:T(8,128)(2,1)} %get-tuple-element.21), channel_id=1, source_target_pairs={{0,3},{1,0},{2,1},{3,2},{4,7},{5,4},{6,5},{7,6},{8,11},{9,8},{10,9... | collective-permute-start | bytes 2359304 | tf_op jit(solution)/shard_map/ppermute | solution.py:15
  7.4 35.7 %collective-permute-start.2 = (bf16[384,1024]{1,0:T(8,128)(2,1)}, bf16[384,1024]{1,0:T(8,128)(2,1)}, u32[]{:S(2)}, u32[]{:S(2)}) collective-permute-start(bf16[384,1024]{1,0:T(8,128)(2,1)} %get-tuple-element.22), channel_id=1, source_target_pairs={{0,2},{1,3},{2,0},{3,1},{4,6},{5,7},{6,4},{7,5},{8,10},{9,11},{10,... | collective-permute-start | bytes 2359304 | tf_op jit(solution)/shard_map/ppermute | solution.py:15
  12.8 40.9 %all-to-all-start = ((bf16[64,8,1024]{2,1,0:T(8,128)(2,1)}), bf16[64,8,1024]{2,1,0:T(8,128)(2,1)}, u32[]{:S(2)}, u32[]{:S(2)}) async-start(bf16[64,8,1024]{2,1,0:T(8,128)(2,1)} %fusion), calls=%async_computation | async-start | bytes 2097152 | tf_op jit(solution)/shard_map/all_to_all | solution.py:185
  53.8 6.7 %copy-start.4 = (bf16[1024,768]{1,0:T(8,128)(2,1)S(1)}, bf16[1024,768]{1,0:T(8,128)(2,1)}, u32[]{:S(2)}) copy-start(bf16[1024,768]{1,0:T(8,128)(2,1)} %pad_maximum_fusion.1) | copy-start | bytes 4718596
  55.2 16.2 %collective-permute-start.3 = (bf16[256,1024]{1,0:T(8,128)(2,1)S(1)}, bf16[256,1024]{1,0:T(8,128)(2,1)S(1)}, u32[]{:S(2)}, u32[]{:S(2)}) collective-permute-start(bf16[256,1024]{1,0:T(8,128)(2,1)S(1)} %get-tuple-element.46), channel_id=1, source_target_pairs={{0,1},{1,2},{2,3},{3,0},{4,5},{5,6},{6,7},{7,4},{8,9},{9,10},{10,1... | collective-permute-start | bytes 1572872 | tf_op jit(solution)/shard_map/ppermute | solution.py:15
  55.9 26.2 %copy-start.3 = (bf16[1024,768]{1,0:T(8,128)(2,1)S(1)}, bf16[1024,768]{1,0:T(8,128)(2,1)}, u32[]{:S(2)}) copy-start(bf16[1024,768]{1,0:T(8,128)(2,1)} %pad_maximum_fusion.3) | copy-start | bytes 4718596
  55.9 15.4 %collective-permute-start.6 = (bf16[256,1024]{1,0:T(8,128)(2,1)S(1)}, bf16[256,1024]{1,0:T(8,128)(2,1)S(1)}, u32[]{:S(2)}, u32[]{:S(2)}) collective-permute-start(bf16[256,1024]{1,0:T(8,128)(2,1)S(1)} %get-tuple-element.47), channel_id=1, source_target_pairs={{0,3},{1,0},{2,1},{3,2},{4,7},{5,4},{6,5},{7,6},{8,11},{9,8},{10,9... | collective-permute-start | bytes 1572872 | tf_op jit(solution)/shard_map/ppermute | solution.py:15
  58.5 23.6 %collective-permute-start.5 = (bf16[256,1024]{1,0:T(8,128)(2,1)S(1)}, bf16[256,1024]{1,0:T(8,128)(2,1)S(1)}, u32[]{:S(2)}, u32[]{:S(2)}) collective-permute-start(bf16[256,1024]{1,0:T(8,128)(2,1)S(1)} %get-tuple-element.46), channel_id=1, source_target_pairs={{0,3},{1,0},{2,1},{3,2},{4,7},{5,4},{6,5},{7,6},{8,11},{9,8},{10,9... | collective-permute-start | bytes 1572872 | tf_op jit(solution)/shard_map/ppermute | solution.py:15
  58.5 24.6 %collective-permute-start.4 = (bf16[256,1024]{1,0:T(8,128)(2,1)S(1)}, bf16[256,1024]{1,0:T(8,128)(2,1)S(1)}, u32[]{:S(2)}, u32[]{:S(2)}) collective-permute-start(bf16[256,1024]{1,0:T(8,128)(2,1)S(1)} %get-tuple-element.47), channel_id=1, source_target_pairs={{0,1},{1,2},{2,3},{3,0},{4,5},{5,6},{6,7},{7,4},{8,9},{9,10},{10,1... | collective-permute-start | bytes 1572872 | tf_op jit(solution)/shard_map/ppermute | solution.py:15
  62.7 20.4 %copy-start.2 = (bf16[1024,768]{1,0:T(8,128)(2,1)S(1)}, bf16[1024,768]{1,0:T(8,128)(2,1)}, u32[]{:S(2)}) copy-start(bf16[1024,768]{1,0:T(8,128)(2,1)} %pad_maximum_fusion.2) | copy-start | bytes 4718596
  71.3 20.3 %collective-permute-start.7 = (bf16[256,1024]{1,0:T(8,128)(2,1)S(1)}, bf16[256,1024]{1,0:T(8,128)(2,1)S(1)}, u32[]{:S(2)}, u32[]{:S(2)}) collective-permute-start(bf16[256,1024]{1,0:T(8,128)(2,1)S(1)} %collective-permute-done.3), channel_id=1, source_target_pairs={{0,1},{1,2},{2,3},{3,0},{4,5},{5,6},{6,7},{7,4},{8,9},{9,10},{10,1... | collective-permute-start | bytes 1572872 | tf_op jit(solution)/shard_map/ppermute | solution.py:15
  71.3 20.3 %collective-permute-start.8 = (bf16[256,1024]{1,0:T(8,128)(2,1)S(1)}, bf16[256,1024]{1,0:T(8,128)(2,1)S(1)}, u32[]{:S(2)}, u32[]{:S(2)}) collective-permute-start(bf16[256,1024]{1,0:T(8,128)(2,1)S(1)} %collective-permute-done.6), channel_id=1, source_target_pairs={{0,3},{1,0},{2,1},{3,2},{4,7},{5,4},{6,5},{7,6},{8,11},{9,8},{10,9... | collective-permute-start | bytes 1572872 | tf_op jit(solution)/shard_map/ppermute | solution.py:15
  91.6 7.6 %copy-start.1 = (bf16[1536,1024]{1,0:T(8,128)(2,1)S(1)}, bf16[1536,1024]{1,0:T(8,128)(2,1)}, u32[]{:S(2)}) copy-start(bf16[1536,1024]{1,0:T(8,128)(2,1)} %pad_maximum_fusion) | copy-start | bytes 9437188
  92.9 16.0 %collective-permute-start.11 = (bf16[256,384]{1,0:T(8,128)(2,1)S(1)}, bf16[256,384]{1,0:T(8,128)(2,1)S(1)}, u32[]{:S(2)}, u32[]{:S(2)}) collective-permute-start(bf16[256,384]{1,0:T(8,128)(2,1)S(1)} %get-tuple-element.48), channel_id=1, source_target_pairs={{0,3},{1,0},{2,1},{3,2},{4,7},{5,4},{6,5},{7,6},{8,11},{9,8},{10,9... | collective-permute-start | bytes 589832 | tf_op jit(solution)/shard_map/ppermute | solution.py:15
  95.9 9.0 %collective-permute-start.9 = (bf16[256,384]{1,0:T(8,128)(2,1)S(1)}, bf16[256,384]{1,0:T(8,128)(2,1)S(1)}, u32[]{:S(2)}, u32[]{:S(2)}) collective-permute-start(bf16[256,384]{1,0:T(8,128)(2,1)S(1)} %get-tuple-element.48), channel_id=1, source_target_pairs={{0,1},{1,2},{2,3},{3,0},{4,5},{5,6},{6,7},{7,4},{8,9},{9,10},{10,1... | collective-permute-start | bytes 589832 | tf_op jit(solution)/shard_map/ppermute | solution.py:15
  95.9 9.0 %collective-permute-start.12 = (bf16[256,384]{1,0:T(8,128)(2,1)S(1)}, bf16[256,384]{1,0:T(8,128)(2,1)S(1)}, u32[]{:S(2)}, u32[]{:S(2)}) collective-permute-start(bf16[256,384]{1,0:T(8,128)(2,1)S(1)} %get-tuple-element.49), channel_id=1, source_target_pairs={{0,3},{1,0},{2,1},{3,2},{4,7},{5,4},{6,5},{7,6},{8,11},{9,8},{10,9... | collective-permute-start | bytes 589832 | tf_op jit(solution)/shard_map/ppermute | solution.py:15
  99.2 9.0 %collective-permute-start.10 = (bf16[256,384]{1,0:T(8,128)(2,1)S(1)}, bf16[256,384]{1,0:T(8,128)(2,1)S(1)}, u32[]{:S(2)}, u32[]{:S(2)}) collective-permute-start(bf16[256,384]{1,0:T(8,128)(2,1)S(1)} %get-tuple-element.49), channel_id=1, source_target_pairs={{0,1},{1,2},{2,3},{3,0},{4,5},{5,6},{6,7},{7,4},{8,9},{9,10},{10,1... | collective-permute-start | bytes 589832 | tf_op jit(solution)/shard_map/ppermute | solution.py:15
  104.9 6.9 %collective-permute-start.13 = (bf16[256,384]{1,0:T(8,128)(2,1)S(1)}, bf16[256,384]{1,0:T(8,128)(2,1)S(1)}, u32[]{:S(2)}, u32[]{:S(2)}) collective-permute-start(bf16[256,384]{1,0:T(8,128)(2,1)S(1)} %collective-permute-done.9), channel_id=1, source_target_pairs={{0,1},{1,2},{2,3},{3,0},{4,5},{5,6},{6,7},{7,4},{8,9},{9,10},{10,1... | collective-permute-start | bytes 589832 | tf_op jit(solution)/shard_map/ppermute | solution.py:15
  104.9 6.9 %collective-permute-start.14 = (bf16[256,384]{1,0:T(8,128)(2,1)S(1)}, bf16[256,384]{1,0:T(8,128)(2,1)S(1)}, u32[]{:S(2)}, u32[]{:S(2)}) collective-permute-start(bf16[256,384]{1,0:T(8,128)(2,1)S(1)} %collective-permute-done.12), channel_id=1, source_target_pairs={{0,3},{1,0},{2,1},{3,2},{4,7},{5,4},{6,5},{7,6},{8,11},{9,8},{10,9... | collective-permute-start | bytes 589832 | tf_op jit(solution)/shard_map/ppermute | solution.py:15
  113.5 8.6 %copy-start.6 = (bf16[32,2048]{1,0:T(8,128)(2,1)S(1)}, bf16[32,2048]{1,0:T(8,128)(2,1)}, u32[]{:S(2)}) copy-start(bf16[32,2048]{1,0:T(8,128)(2,1)} %param.23) | copy-start | bytes 393220
  113.5 8.6 %copy-start.12 = (bf16[1,128,128]{2,1,0:T(8,128)(2,1)S(1)}, bf16[1,128,128]{2,1,0:T(8,128)(2,1)}, u32[]{:S(2)}) copy-start(bf16[1,128,128]{2,1,0:T(8,128)(2,1)} %param.24) | copy-start | bytes 98308
  113.5 36.7 %copy-start.9 = (bf16[512,32]{0,1:T(8,128)(2,1)S(1)}, bf16[512,32]{0,1:T(8,128)(2,1)}, u32[]{:S(2)}) copy-start(bf16[512,32]{0,1:T(8,128)(2,1)} %get-tuple-element.32) | copy-start | bytes 98308
  113.5 36.7 %all-to-all-start.1 = ((bf16[64,8,1024]{2,1,0:T(8,128)(2,1)}), bf16[64,8,1024]{2,1,0:T(8,128)(2,1)S(1)}, u32[]{:S(2)}, u32[]{:S(2)}) async-start(bf16[64,8,1024]{2,1,0:T(8,128)(2,1)} %fusion.1), calls=%async_computation.1 | async-start | bytes 2097152 | tf_op jit(solution)/shard_map/all_to_all | solution.py:199
  121.5 34.5 %copy-start.13 = (f32[32,32]{1,0:T(8,128)S(1)}, f32[32,32]{1,0:T(8,128)}, u32[]{:S(2)}) copy-start(f32[32,32]{1,0:T(8,128)} %shard_map.165) | copy-start | bytes 12292
  150.3 12.7 %copy-start.10 = (f32[4096]{0:T(1024)S(1)}, f32[4096]{0:T(1024)}, u32[]{:S(2)}) copy-start(f32[4096]{0:T(1024)} %param.20) | copy-start | bytes 49156
  150.6 12.7 %copy-start.8 = (bf16[32,1024]{1,0:T(8,128)(2,1)}, bf16[32,1024]{1,0:T(8,128)(2,1)S(1)}, u32[]{:S(2)}) copy-start(bf16[32,1024]{1,0:T(8,128)(2,1)S(1)} %fusion.47) | copy-start | bytes 196612
  151.3 12.0 %copy-start.5 = (bf16[4096,128]{1,0:T(8,128)(2,1)S(1)}, bf16[4096,128]{1,0:T(8,128)(2,1)}, u32[]{:S(2)}) copy-start(bf16[4096,128]{1,0:T(8,128)(2,1)} %param.21) | copy-start | bytes 3145732
  151.3 11.3 %all-to-all-start.2 = ((bf16[4,32,1024]{2,1,0:T(8,128)(2,1)}), bf16[4,32,1024]{2,1,0:T(8,128)(2,1)S(1)}, u32[]{:S(2)}, u32[]{:S(2)}) async-start(bf16[4,32,1024]{2,1,0:T(8,128)(2,1)} %broadcast_in_dim.78), calls=%async_computation.2 | async-start | bytes 524288 | tf_op jit(solution)/shard_map/all_to_all | solution.py:58
  162.9 1.4 copy-start.17
  163.3 1.7 %copy-start.15 = (bf16[32,128]{1,0:T(8,128)(2,1)}, bf16[32,128]{1,0:T(8,128)(2,1)S(1)}, u32[]{:S(2)}) copy-start(bf16[32,128]{1,0:T(8,128)(2,1)S(1)} %convolution_convert_fusion.1) | copy-start | bytes 24580
  163.7 2.1 %copy-start.11 = (bf16[32,128]{1,0:T(8,128)(2,1)}, bf16[32,128]{1,0:T(8,128)(2,1)S(1)}, u32[]{:S(2)}) copy-start(bf16[32,128]{1,0:T(8,128)(2,1)S(1)} %convolution_convert_fusion.2) | copy-start | bytes 24580

commit v3 on v2

--- a/solution.py
+++ b/solution.py
@@ -4,9 +4,11 @@
 import jax.numpy as jnp
 from jax import lax
 from jax.experimental import pallas as pl
+from jax.experimental.pallas import tpu as pltpu
 from jax.sharding import PartitionSpec as P
 
 HEAD_SIZE = 128
+EXPERT_COLUMNS = 64
 CHUNKS = 1
 
 
@@ -26,6 +28,55 @@
     return rows, before, after, opposite
 
 
+def routed_kernel(routes_ref, scores_ref, hidden_ref, sent_ref, combine_ref):
+    top_count, token_count = routes_ref.shape
+    slot_total = sent_ref.shape[0]
+    capacity = slot_total // EXPERT_COLUMNS
+    routes = routes_ref[...]
+    weights = scores_ref[...] / jnp.sum(scores_ref[...], axis=0, keepdims=True)
+    expert = lax.broadcasted_iota(jnp.int32, (EXPERT_COLUMNS, token_count), 0)
+    member = jnp.zeros((EXPERT_COLUMNS, token_count), jnp.float32)
+    portion = jnp.zeros((EXPERT_COLUMNS, token_count), jnp.float32)
+    for k in range(top_count):
+        named = routes[k : k + 1, :] == expert
+        member = jnp.where(named, 1.0, member)
+        portion = jnp.where(named, weights[k : k + 1, :], portion)
+    earlier = lax.broadcasted_iota(jnp.int32, (token_count, token_count), 0) < lax.broadcasted_iota(
+        jnp.int32, (token_count, token_count), 1
+    )
+    earlier = jnp.where(earlier, 1.0, 0.0).astype(jnp.bfloat16)
+    rank = jnp.dot(member.astype(jnp.bfloat16), earlier, preferred_element_type=jnp.float32)
+    key = jnp.where(member > 0.5, rank, -1.0)
+    upper = portion.astype(jnp.bfloat16).astype(jnp.float32)
+    lower = portion - upper
+    slot = lax.broadcasted_iota(jnp.int32, (slot_total, EXPERT_COLUMNS), 0)
+    first = lax.broadcasted_iota(jnp.int32, (slot_total, EXPERT_COLUMNS), 1) * capacity
+    of_expert = jnp.where((slot >= first) & (slot < first + capacity), 1.0, 0.0).astype(jnp.bfloat16)
+    table = jnp.concatenate([key, upper, lower], axis=1).astype(jnp.bfloat16)
+    spread = jnp.dot(of_expert, table, preferred_element_type=jnp.float32)
+    place = lax.rem(lax.broadcasted_iota(jnp.int32, (slot_total, token_count), 0), capacity)
+    chosen = jnp.where(spread[:, :token_count] == place.astype(jnp.float32), 1.0, 0.0)
+    sent_ref[...] = jnp.dot(
+        chosen.astype(jnp.bfloat16), hidden_ref[...], preferred_element_type=jnp.float32
+    ).astype(sent_ref.dtype)
+    both = jnp.concatenate([chosen, chosen], axis=1)
+    combine_ref[...] = (both * spread[:, token_count:]).astype(combine_ref.dtype)
+
+
+def routed_rows(routes, scores, hidden, capacity):
+    slot_total = EXPERT_COLUMNS * capacity
+    token_count, width = hidden.shape
+    return pl.pallas_call(
+        routed_kernel,
+        out_shape=[
+            jax.ShapeDtypeStruct((slot_total, width), hidden.dtype),
+            jax.ShapeDtypeStruct((slot_total, 2 * token_count), jnp.bfloat16),
+        ],
+        compiler_params=pltpu.CompilerParams(vmem_limit_bytes=12 << 20),
+        cost_estimate=pl.CostEstimate(flops=1 << 26, bytes_accessed=3 * slot_total * width, transcendentals=0),
+    )(routes.T, scores.T, hidden)
+
+
 def around(value, dim, size):
     index = lax.axis_index("tp")
     count = lax.axis_size("tp")
@@ -62,24 +113,26 @@
     return joined_along(copy_for_each(shard, axis), dim)
 
 
-def ancestry_kernel(parents_ref, related_ref):
-    node_count = parents_ref.shape[0]
+def parent_kernel(parents_ref, reached_ref):
+    node_count = parents_ref.shape[1]
+    row = lax.broadcasted_iota(jnp.int32, (node_count, node_count), 0)
     column = lax.broadcasted_iota(jnp.int32, (node_count, node_count), 1)
-    row = lax.broadcasted_iota(jnp.int32, (node_count, node_count), 0)
-    reached = jnp.where((parents_ref[...] == column) | (row == column), 1.0, 0.0)
-    for doubling in range((node_count - 1).bit_length()):
-        product = jnp.dot(reached, reached, preferred_element_type=jnp.float32)
-        reached = jnp.minimum(product, 1.0)
-    related_ref[...] = reached
-
-
-def ancestry(parents):
+    reached_ref[...] = jnp.where((parents_ref[...] == row) | (row == column), 1.0, 0.0)
+
+
+def own_and_parents(parents):
     node_count = parents.shape[1]
     return pl.pallas_call(
-        ancestry_kernel,
+        parent_kernel,
         out_shape=jax.ShapeDtypeStruct((node_count, node_count), jnp.float32),
         cost_estimate=pl.CostEstimate(flops=23070000000, bytes_accessed=8192, transcendentals=0),
-    )(parents.reshape(node_count, 1))
+    )(parents)
+
+
+def ancestry(reached):
+    for doubling in range((reached.shape[0] - 1).bit_length()):
+        reached = jnp.minimum(jnp.dot(reached, reached, preferred_element_type=jnp.float32), 1.0)
+    return reached.T
 
 
 def attend_local(
@@ -157,35 +210,26 @@
     expert_count = lax.axis_size("dp")
     capacity = min(token_count, 2 * token_count * top_count // expert_count)
     column_count = hidden.shape[1]
-    down_own, *down_sent = around(w_down[0], 1, column_count)
-    routes, routing_weights, down_sent = lax.optimization_barrier((routes, routing_weights, down_sent))
-    weights = routing_weights / jnp.sum(routing_weights, axis=1, keepdims=True)
-    expert_ids = jnp.arange(expert_count, dtype=jnp.int32)
-    chosen = routes[:, :, None] == expert_ids[None, None, :]
-    member = jnp.any(chosen, axis=1)
-    portion = jnp.sum(jnp.where(chosen, weights[:, :, None], 0.0), axis=1)
-    earlier = jnp.tril(jnp.ones((token_count, token_count), jnp.bfloat16), -1)
-    rank = jnp.dot(earlier, member.astype(jnp.bfloat16), preferred_element_type=jnp.float32)
-    slots = jnp.arange(capacity, dtype=jnp.float32)
-    placed = member.T[:, None, :] & (rank.T[:, None, :] == slots[None, :, None])
-    placed = placed.reshape(expert_count * capacity, token_count)
-    outgoing = jnp.dot(
-        placed.astype(jnp.bfloat16), hidden, preferred_element_type=jnp.float32
-    ).astype(jnp.bfloat16)
+    to_opposite = around(w_down[0], 1, column_count)[3]
+    routes, routing_weights, to_opposite = lax.optimization_barrier((routes, routing_weights, to_opposite))
+    outgoing, both = routed_rows(routes, routing_weights, hidden, capacity)
     outgoing = outgoing.reshape(expert_count, capacity, column_count)
-    down_received = sent_around(down_sent)
-    down_whole = jnp.concatenate([down_own, *down_received], axis=0)
-    down_whole, parents = lax.optimization_barrier((down_whole, parents))
-    related = ancestry(parents)
+    outgoing, w_down = lax.optimization_barrier((outgoing, w_down))
+    down_own, to_before, to_after, _ = around(w_down[0], 1, column_count)
+    before, after, opposite = sent_around((to_before, to_after, to_opposite))
+    opposite, parents = lax.optimization_barrier((opposite, parents))
+    reached = own_and_parents(parents)
     hidden_units = w_gate.shape[2]
     both_weights = [
         jnp.concatenate(pair, axis=1)
         for pair in zip(around(w_gate[0], 0, column_count), around(w_up[0], 0, column_count))
     ]
     received = lax.all_to_all(outgoing, "dp", split_axis=0, concat_axis=0, tiled=True)
-    received, down_whole, both_weights, related = lax.optimization_barrier(
-        (received, down_whole, both_weights, related)
-    )
+    received, before, after, opposite, both_weights, reached = lax.optimization_barrier(
+        (received, before, after, opposite, both_weights, reached)
+    )
+    down_whole = jnp.concatenate([down_own, before, after, opposite], axis=0)
+    related = ancestry(reached)
     down_blocks = jnp.split(down_whole, lax.axis_size("tp"))
     chunk = capacity // CHUNKS
     returned = []
@@ -201,11 +245,6 @@
             )
         )
     flat_back = jnp.concatenate(returned, axis=1).reshape(expert_count * capacity, column_count)
-    spread = jnp.broadcast_to(portion.T[:, None, :], (expert_count, capacity, token_count))
-    spread = jnp.where(placed, spread.reshape(expert_count * capacity, token_count), 0.0)
-    upper = spread.astype(jnp.bfloat16)
-    lower = (spread - upper.astype(jnp.float32)).astype(jnp.bfloat16)
-    both = jnp.concatenate([upper, lower], axis=1)
     mixed = lax.dot_general(
         both, flat_back, (((0,), (0,)), ((), ())), preferred_element_type=jnp.float32
     )

time: 166 us -> 162 us (0.976)
  other arithmetic: 8.9 us -> 4.84 us
  waiting for transfers between devices: 80 us -> 76.6 us
  matrix products: 12.8 us -> 15.3 us
    concatenate x1 -> x0, other arithmetic: 3.08 us -> none  [on_device(): down_whole = jnp.concatenate([down_own, *down_received], axis=0)]
    ppermute x15, waiting for transfers between devices: 41.3 us -> 38.7 us  [shifted(): lax.ppermute(value, 'tp', [(i, (i + step) % size) for i in range(size)])]
    dot_general x6, matrix products: 6.14 us -> 8.39 us  [summed_products(): total = total + jnp.dot(block, weight, preferred_element_type=jnp.float32)]
    unnamed x37 -> x35, local copies, waits for them, and re-layouts: 0.78 us -> 2.97 us
    dynamic_slice x2 -> x3, local copies, waits for them, and re-layouts: 6.85 us -> 8.33 us  [around(): lax.dynamic_slice_in_dim(value, (index + step) % count * size, size, dim)]
  transfers between devices with their start and end apart: 18 -> 18, of which waited for: 10 -> 10; matrix products, arithmetic and copies ran while one was open for 13% -> 13% of each run, Pallas kernels for 1% -> 2%
where the time goes in v3:
time: 162 us
  waiting for transfers between devices  76.6 us (47%)
  starting transfers between devices  46.6 us (29%)
  matrix products  15.3 us (9%)
  local copies, waits for them, and re-layouts  13.7 us (8%)
  other arithmetic  4.84 us (3%)
  Pallas kernels  2.96 us (2%)
  between operations  1.72 us (1%)
    ppermute x15, waiting for transfers between devices, shifted(): lax.ppermute(value, 'tp', [(i, (i + step) % size) for i in range(size)])  38.7 us
    all_to_all x1, waiting for transfers between devices, on_device(): lax.all_to_all(made.reshape(expert_count, chunk, column_count), 'dp', spl...  27.4 us
    ppermute x15, starting transfers between devices, shifted(): lax.ppermute(value, 'tp', [(i, (i + step) % size) for i in range(size)])  23.3 us
    all_to_all x1, starting transfers between devices, on_device(): lax.all_to_all(outgoing, 'dp', split_axis=0, concat_axis=0, tiled=True)  12.2 us
    dot_general x6, matrix products, summed_products(): total = total + jnp.dot(block, weight, preferred_element_type=jnp.float32)  8.39 us
    dynamic_slice x3, local copies, waits for them, and re-layouts, around(): lax.dynamic_slice_in_dim(value, (index + step) % count * size, size, dim)  8.33 us
    all_to_all x1, starting transfers between devices, on_device(): lax.all_to_all(made.reshape(expert_count, chunk, column_count), 'dp', spl...  7.3 us
    all_to_all x1, waiting for transfers between devices, copy_for_each(): return lax.all_to_all(copies, axis, split_axis=0, concat_axis=0, tiled=True)  6.3 us
  transfers between devices with their start and end apart: 18, of which 10 were waited for; matrix products, arithmetic and copies ran while one was open for 13% of the time, Pallas kernels for 2%

profile of v3, /device:TPU:2, one launch (start us, length us, event | category | flops | bytes accessed | tf_op | source)
XLA Modules:
  0.0 161.6 jit_solution(18009091211803778811)
XLA Ops:
  0.7 2.2 %dynamic-slice_bitcast_fusion.10 = bf16[384,1024]{1,0:T(8,128)(2,1)} fusion(bf16[1,384,4096]{2,1,0:T(8,128)(2,1)} %param.19, s32[]{:T(128)S(6)} %select_n.67), kind=kLoop, calls=%fused_computation.56 | loop fusion | bytes 1572868 | tf_op jit(solution)/shard_map/dynamic_slice | solution.py:84
  2.9 3.2 %collective-permute-start.2 = (bf16[384,1024]{1,0:T(8,128)(2,1)}, bf16[384,1024]{1,0:T(8,128)(2,1)S(1)}, u32[]{:S(2)}, u32[]{:S(2)}) collective-permute-start(bf16[384,1024]{1,0:T(8,128)(2,1)} %dynamic-slice_bitcast_fusion.10), channel_id=1, source_target_pairs={{0,2},{1,3},{2,0},{3,1},{4,6},{5,7},{6,4},{7,5},{8,10},{9,11},{10,... | collective-permute-start | bytes 2359304 | tf_op jit(solution)/shard_map/ppermute | solution.py:17
  6.1 0.8 copy-done.1
  6.9 0.7 copy-done.3
  7.6 0.7 copy-done.4
  8.3 1.7 %shard_map.165 = (bf16[512,1024]{1,0:T(8,128)(2,1)}, bf16[512,64]{1,0:T(8,128)(2,1)S(1)}) custom-call(s32[8,32]{1,0:T(8,128)S(1)} %bitcast.129, f32[8,32]{1,0:T(8,128)S(1)} %bitcast.130, bf16[32,1024]{1,0:T(8,128)(2,1)S(1)} %copy-done.1), custom_call_target="tpu_custom_call" | custom-call | flops 67108864 | bytes 1572864 | tf_op jit(solution)/shard_map/pallas_call | solution.py:69
  10.0 12.2 %all-to-all-start = ((bf16[64,8,1024]{2,1,0:T(8,128)(2,1)}), bf16[64,8,1024]{2,1,0:T(8,128)(2,1)}, u32[]{:S(2)}, u32[]{:S(2)}) async-start(bf16[64,8,1024]{2,1,0:T(8,128)(2,1)} %bitcast.3), calls=%async_computation | async-start | bytes 2097152 | tf_op jit(solution)/shard_map/all_to_all | solution.py:227
  22.3 2.6 %dynamic-slice_bitcast_fusion.8 = (bf16[384,1024]{1,0:T(8,128)(2,1)}, bf16[384,1024]{1,0:T(8,128)(2,1)}) fusion(bf16[1,384,4096]{2,1,0:T(8,128)(2,1)} %param.19, s32[]{:T(128)S(6)} %select_n.71, s32[]{:T(128)S(6)} %select_n.69), kind=kLoop, calls=%fused_computation.54 | loop fusion | bytes 3145736 | tf_op jit(solution)/shard_map/dynamic_slice | solution.py:84
  24.9 1.1 collective-permute-start.1
  26.0 1.0 collective-permute-start
  26.9 3.4 %dynamic-slice_bitcast_fusion = (bf16[1024,384]{1,0:T(8,128)(2,1)S(1)}, bf16[1024,384]{1,0:T(8,128)(2,1)S(1)}, bf16[1024,384]{1,0:T(8,128)(2,1)S(1)}, bf16[1024,...) fusion(bf16[1,4096,384]{2,1,0:T(8,128)(2,1)} %param.18, ...), kind=kLoop, calls=%fused_computation.46 | loop fusion | bytes 12582928 | tf_op jit(solution)/shard_map/dynamic_slice | solution.py:84
  30.5 1.3 pad_maximum_fusion.1
  31.8 1.3 pad_maximum_fusion
  33.1 1.3 pad_maximum_fusion.2
  34.4 1.3 shard_map.166
  35.7 9.1 %collective-permute-done.1 = bf16[384,1024]{1,0:T(8,128)(2,1)} collective-permute-done((bf16[384,1024]{1,0:T(8,128)(2,1)}, bf16[384,1024]{1,0:T(8,128)(2,1)}, u32[]{:S(2)}, u32[]{:S(2)}) %collective-permute-start.1) | collective-permute-done | bytes 786464 | tf_op jit(solution)/shard_map/ppermute | solution.py:17
  44.8 2.0 %collective-permute-done = bf16[384,1024]{1,0:T(8,128)(2,1)} collective-permute-done((bf16[384,1024]{1,0:T(8,128)(2,1)}, bf16[384,1024]{1,0:T(8,128)(2,1)}, u32[]{:S(2)}, u32[]{:S(2)}) %collective-permute-start) | collective-permute-done | bytes 786464 | tf_op jit(solution)/shard_map/ppermute | solution.py:17
  46.8 4.1 %all-to-all-done = bf16[64,8,1024]{2,1,0:T(8,128)(2,1)} async-done(((bf16[64,8,1024]{2,1,0:T(8,128)(2,1)}), bf16[64,8,1024]{2,1,0:T(8,128)(2,1)}, u32[]{:S(2)}, u32[]{:S(2)}) %all-to-all-start) | async-done | bytes 1048608 | tf_op jit(solution)/shard_map/all_to_all | solution.py:227
  50.9 1.4 slice_bitcast_fusion.1
  52.3 0.8 collective-permute-start.3
  53.1 2.6 %collective-permute-start.6 = (bf16[256,1024]{1,0:T(8,128)(2,1)S(1)}, bf16[256,1024]{1,0:T(8,128)(2,1)S(1)}, u32[]{:S(2)}, u32[]{:S(2)}) collective-permute-start(bf16[256,1024]{1,0:T(8,128)(2,1)S(1)} %get-tuple-element.51), channel_id=1, source_target_pairs={{0,3},{1,0},{2,1},{3,2},{4,7},{5,4},{6,5},{7,6},{8,11},{9,8},{10,9... | collective-permute-start | bytes 1572872 | tf_op jit(solution)/shard_map/ppermute | solution.py:17
  55.7 2.0 %collective-permute-start.4 = (bf16[256,1024]{1,0:T(8,128)(2,1)S(1)}, bf16[256,1024]{1,0:T(8,128)(2,1)S(1)}, u32[]{:S(2)}, u32[]{:S(2)}) collective-permute-start(bf16[256,1024]{1,0:T(8,128)(2,1)S(1)} %get-tuple-element.51), channel_id=1, source_target_pairs={{0,1},{1,2},{2,3},{3,0},{4,5},{5,6},{6,7},{7,4},{8,9},{9,10},{10,1... | collective-permute-start | bytes 1572872 | tf_op jit(solution)/shard_map/ppermute | solution.py:17
  57.7 2.2 %fusion.22 = f32[512,768]{1,0:T(8,128)S(1)} fusion(bf16[1024,768]{1,0:T(8,128)(2,1)S(1)} %copy-done.7, bf16[64,8,1024]{2,1,0:T(8,128)(2,1)} %all-to-all-done), kind=kOutput, calls=%fused_computation.39 | convolution fusion | flops 805306368 | bytes 4194304 | tf_op jit(solution)/shard_map/dot_general | solution.py:95
  59.9 8.6 %collective-permute-done.3 = bf16[256,1024]{1,0:T(8,128)(2,1)S(1)} collective-permute-done((bf16[256,1024]{1,0:T(8,128)(2,1)S(1)}, bf16[256,1024]{1,0:T(8,128)(2,1)S(1)}, u32[]{:S(2)}, u32[]{:S(2)}) %collective-permute-start.3) | collective-permute-done | bytes 524320 | tf_op jit(solution)/shard_map/ppermute | solution.py:17
  68.5 3.2 %collective-permute-start.8 = (bf16[256,1024]{1,0:T(8,128)(2,1)S(1)}, bf16[256,1024]{1,0:T(8,128)(2,1)S(1)}, u32[]{:S(2)}, u32[]{:S(2)}) collective-permute-start(bf16[256,1024]{1,0:T(8,128)(2,1)S(1)} %collective-permute-done.6), channel_id=1, source_target_pairs={{0,3},{1,0},{2,1},{3,2},{4,7},{5,4},{6,5},{7,6},{8,11},{9,8},{10,9... | collective-permute-start | bytes 1572872 | tf_op jit(solution)/shard_map/ppermute | solution.py:17
  71.7 7.5 %collective-permute-done.5 = bf16[256,1024]{1,0:T(8,128)(2,1)S(1)} collective-permute-done((bf16[256,1024]{1,0:T(8,128)(2,1)S(1)}, bf16[256,1024]{1,0:T(8,128)(2,1)S(1)}, u32[]{:S(2)}, u32[]{:S(2)}) %collective-permute-start.5) | collective-permute-done | bytes 524320 | tf_op jit(solution)/shard_map/ppermute | solution.py:17
  79.3 1.0 fusion.13
  80.3 1.0 fusion.9
  81.3 7.5 %collective-permute-done.7 = bf16[256,1024]{1,0:T(8,128)(2,1)S(1)} collective-permute-done((bf16[256,1024]{1,0:T(8,128)(2,1)S(1)}, bf16[256,1024]{1,0:T(8,128)(2,1)S(1)}, u32[]{:S(2)}, u32[]{:S(2)}) %collective-permute-start.7) | collective-permute-done | bytes 524320 | tf_op jit(solution)/shard_map/ppermute | solution.py:17
  88.8 1.0 add_add_fusion
  90.1 3.0 %collective-permute-start.11 = (bf16[256,384]{1,0:T(8,128)(2,1)S(1)}, bf16[256,384]{1,0:T(8,128)(2,1)S(1)}, u32[]{:S(2)}, u32[]{:S(2)}) collective-permute-start(bf16[256,384]{1,0:T(8,128)(2,1)S(1)} %get-tuple-element.52), channel_id=1, source_target_pairs={{0,3},{1,0},{2,1},{3,2},{4,7},{5,4},{6,5},{7,6},{8,11},{9,8},{10,9... | collective-permute-start | bytes 589832 | tf_op jit(solution)/shard_map/ppermute | solution.py:17
  93.1 3.2 %collective-permute-start.12 = (bf16[256,384]{1,0:T(8,128)(2,1)S(1)}, bf16[256,384]{1,0:T(8,128)(2,1)S(1)}, u32[]{:S(2)}, u32[]{:S(2)}) collective-permute-start(bf16[256,384]{1,0:T(8,128)(2,1)S(1)} %get-tuple-element.53), channel_id=1, source_target_pairs={{0,3},{1,0},{2,1},{3,2},{4,7},{5,4},{6,5},{7,6},{8,11},{9,8},{10,9... | collective-permute-start | bytes 589832 | tf_op jit(solution)/shard_map/ppermute | solution.py:17
  96.3 1.8 %fusion.25 = f32[512,1024]{1,0:T(8,128)S(1)} fusion(bf16[512,384]{1,0:T(8,128)(2,1)S(1)} %fusion.24, bf16[1,384,4096]{2,1,0:T(8,128)(2,1)} %param.19, s32[]{:T(128)S(6)} %select_n.73), kind=kOutput, calls=%fused_computation.43 | convolution fusion | flops 402653184 | bytes 3276804 | tf_op jit(solution)/shard_map/dot_general | solution.py:95
  98.2 3.9 %collective-permute-done.9 = bf16[256,384]{1,0:T(8,128)(2,1)S(1)} collective-permute-done((bf16[256,384]{1,0:T(8,128)(2,1)S(1)}, bf16[256,384]{1,0:T(8,128)(2,1)S(1)}, u32[]{:S(2)}, u32[]{:S(2)}) %collective-permute-start.9) | collective-permute-done | bytes 196640 | tf_op jit(solution)/shard_map/ppermute | solution.py:17
  102.1 3.2 %collective-permute-start.14 = (bf16[256,384]{1,0:T(8,128)(2,1)S(1)}, bf16[256,384]{1,0:T(8,128)(2,1)S(1)}, u32[]{:S(2)}, u32[]{:S(2)}) collective-permute-start(bf16[256,384]{1,0:T(8,128)(2,1)S(1)} %collective-permute-done.12), channel_id=1, source_target_pairs={{0,3},{1,0},{2,1},{3,2},{4,7},{5,4},{6,5},{7,6},{8,11},{9,8},{10,9... | collective-permute-start | bytes 589832 | tf_op jit(solution)/shard_map/ppermute | solution.py:17
  105.4 1.8 %fusion.29 = f32[512,1024]{1,0:T(8,128)S(1)} fusion(bf16[384,1024]{1,0:T(8,128)(2,1)} %collective-permute-done, bf16[256,384]{1,0:T(8,128)(2,1)S(1)} %collective-permute-done.10, bf16[256,384]{1,0:T(8,128)(2,1)S(1)} %collective-permute-done.9), kind=kOutput, calls=%fused_computation.63 | convolution fusion | flops 403439616 | bytes 3276800 | tf_op jit(solution)/shard_map/dot_general | solution.py:97
  107.2 1.8 %fusion.33 = f32[512,1024]{1,0:T(8,128)S(1)} fusion(bf16[384,1024]{1,0:T(8,128)(2,1)} %collective-permute-done.1, bf16[256,384]{1,0:T(8,128)(2,1)S(1)} %collective-permute-done.12, bf16[256,384]{1,0:T(8,128)(2,1)S(1)} %collective-permute-done.11), kind=kOutput, calls=%fused_computation.67 | convolution fusion | flops 403439616 | bytes 3276800 | tf_op jit(solution)/shard_map/dot_general | solution.py:97
  109.1 1.7 %fusion = bf16[64,8,1024]{2,1,0:T(8,128)(2,1)} fusion(bf16[384,1024]{1,0:T(8,128)(2,1)S(1)} %collective-permute-done.2, f32[512,1024]{1,0:T(8,128)S(1)} %fusion.33, f32[512,1024]{1,0:T(8,128)S(1)} %fusion.25, f32[512,1024]{1,0:T(8,128)S(1)} %fusion.29, bf16[256,384]{1,0:T(8,128)(2,1)S(1)} %collective-permute-done.14, ...), kind=kOutput, calls=%fused_computation.6 | convolution fusion | flops 405536768 | bytes 8519680 | tf_op jit(solution)/shard_map/dot_general | solution.py:97
  110.9 7.3 %all-to-all-start.1 = ((bf16[64,8,1024]{2,1,0:T(8,128)(2,1)}), bf16[64,8,1024]{2,1,0:T(8,128)(2,1)S(1)}, u32[]{:S(2)}, u32[]{:S(2)}) async-start(bf16[64,8,1024]{2,1,0:T(8,128)(2,1)} %fusion), calls=%async_computation.1 | async-start | bytes 2097152 | tf_op jit(solution)/shard_map/all_to_all | solution.py:243
  119.5 27.4 %all-to-all-done.1 = bf16[64,8,1024]{2,1,0:T(8,128)(2,1)S(1)} async-done(((bf16[64,8,1024]{2,1,0:T(8,128)(2,1)}), bf16[64,8,1024]{2,1,0:T(8,128)(2,1)S(1)}, u32[]{:S(2)}, u32[]{:S(2)}) %all-to-all-start.1) | async-done | bytes 1048608 | tf_op jit(solution)/shard_map/all_to_all | solution.py:243
  147.3 0.7 broadcast_in_dim.36
  148.1 3.8 %all-to-all-start.2 = ((bf16[4,32,1024]{2,1,0:T(8,128)(2,1)}), bf16[4,32,1024]{2,1,0:T(8,128)(2,1)S(1)}, u32[]{:S(2)}, u32[]{:S(2)}) async-start(bf16[4,32,1024]{2,1,0:T(8,128)(2,1)} %broadcast_in_dim.36), calls=%async_computation.2 | async-start | bytes 524288 | tf_op jit(solution)/shard_map/all_to_all | solution.py:109
  152.3 6.3 %all-to-all-done.2 = bf16[4,32,1024]{2,1,0:T(8,128)(2,1)S(1)} async-done(((bf16[4,32,1024]{2,1,0:T(8,128)(2,1)}), bf16[4,32,1024]{2,1,0:T(8,128)(2,1)S(1)}, u32[]{:S(2)}, u32[]{:S(2)}) %all-to-all-start.2) | async-done | bytes 262176 | tf_op jit(solution)/shard_map/all_to_all | solution.py:109
  158.9 0.3 convolution_convert_fusion
  159.2 0.3 convolution_convert_fusion.1
  159.6 0.3 fusion.69
  160.3 0.3 convolution_bitcast_fusion
  161.0 0.7 copy.50
  (66 shorter events, 2.9 us)
Async XLA Ops:
  0.6 158.2 %copy-start = (bf16[4096,128]{1,0:T(8,128)(2,1)S(1)}, bf16[4096,128]{1,0:T(8,128)(2,1)}, u32[]{:S(2)}) copy-start(bf16[4096,128]{1,0:T(8,128)(2,1)} %param.22) | copy-start | bytes 3145732
  2.9 31.5 %collective-permute-start.2 = (bf16[384,1024]{1,0:T(8,128)(2,1)}, bf16[384,1024]{1,0:T(8,128)(2,1)S(1)}, u32[]{:S(2)}, u32[]{:S(2)}) collective-permute-start(bf16[384,1024]{1,0:T(8,128)(2,1)} %dynamic-slice_bitcast_fusion.10), channel_id=1, source_target_pairs={{0,2},{1,3},{2,0},{3,1},{4,6},{5,7},{6,4},{7,5},{8,10},{9,11},{10,... | collective-permute-start | bytes 2359304 | tf_op jit(solution)/shard_map/ppermute | solution.py:17
  6.1 0.8 copy-start.1
  6.9 0.7 copy-start.3
  7.6 0.7 copy-start.4
  10.0 40.9 %all-to-all-start = ((bf16[64,8,1024]{2,1,0:T(8,128)(2,1)}), bf16[64,8,1024]{2,1,0:T(8,128)(2,1)}, u32[]{:S(2)}, u32[]{:S(2)}) async-start(bf16[64,8,1024]{2,1,0:T(8,128)(2,1)} %bitcast.3), calls=%async_computation | async-start | bytes 2097152 | tf_op jit(solution)/shard_map/all_to_all | solution.py:227
  24.9 19.9 %collective-permute-start.1 = (bf16[384,1024]{1,0:T(8,128)(2,1)}, bf16[384,1024]{1,0:T(8,128)(2,1)}, u32[]{:S(2)}, u32[]{:S(2)}) collective-permute-start(bf16[384,1024]{1,0:T(8,128)(2,1)} %get-tuple-element.48), channel_id=1, source_target_pairs={{0,3},{1,0},{2,1},{3,2},{4,7},{5,4},{6,5},{7,6},{8,11},{9,8},{10,9... | collective-permute-start | bytes 2359304 | tf_op jit(solution)/shard_map/ppermute | solution.py:17
  26.0 20.8 %collective-permute-start = (bf16[384,1024]{1,0:T(8,128)(2,1)}, bf16[384,1024]{1,0:T(8,128)(2,1)}, u32[]{:S(2)}, u32[]{:S(2)}) collective-permute-start(bf16[384,1024]{1,0:T(8,128)(2,1)} %get-tuple-element.49), channel_id=1, source_target_pairs={{0,1},{1,2},{2,3},{3,0},{4,5},{5,6},{6,7},{7,4},{8,9},{9,10},{10,1... | collective-permute-start | bytes 2359304 | tf_op jit(solution)/shard_map/ppermute | solution.py:17
  50.9 6.7 %copy-start.7 = (bf16[1024,768]{1,0:T(8,128)(2,1)S(1)}, bf16[1024,768]{1,0:T(8,128)(2,1)}, u32[]{:S(2)}) copy-start(bf16[1024,768]{1,0:T(8,128)(2,1)} %pad_maximum_fusion) | copy-start | bytes 4718596
  52.3 16.2 %collective-permute-start.3 = (bf16[256,1024]{1,0:T(8,128)(2,1)S(1)}, bf16[256,1024]{1,0:T(8,128)(2,1)S(1)}, u32[]{:S(2)}, u32[]{:S(2)}) collective-permute-start(bf16[256,1024]{1,0:T(8,128)(2,1)S(1)} %get-tuple-element.50), channel_id=1, source_target_pairs={{0,1},{1,2},{2,3},{3,0},{4,5},{5,6},{6,7},{7,4},{8,9},{9,10},{10,1... | collective-permute-start | bytes 1572872 | tf_op jit(solution)/shard_map/ppermute | solution.py:17
  53.1 26.2 %copy-start.6 = (bf16[1024,768]{1,0:T(8,128)(2,1)S(1)}, bf16[1024,768]{1,0:T(8,128)(2,1)}, u32[]{:S(2)}) copy-start(bf16[1024,768]{1,0:T(8,128)(2,1)} %pad_maximum_fusion.2) | copy-start | bytes 4718596
  53.1 15.4 %collective-permute-start.6 = (bf16[256,1024]{1,0:T(8,128)(2,1)S(1)}, bf16[256,1024]{1,0:T(8,128)(2,1)S(1)}, u32[]{:S(2)}, u32[]{:S(2)}) collective-permute-start(bf16[256,1024]{1,0:T(8,128)(2,1)S(1)} %get-tuple-element.51), channel_id=1, source_target_pairs={{0,3},{1,0},{2,1},{3,2},{4,7},{5,4},{6,5},{7,6},{8,11},{9,8},{10,9... | collective-permute-start | bytes 1572872 | tf_op jit(solution)/shard_map/ppermute | solution.py:17
  55.7 23.6 %collective-permute-start.5 = (bf16[256,1024]{1,0:T(8,128)(2,1)S(1)}, bf16[256,1024]{1,0:T(8,128)(2,1)S(1)}, u32[]{:S(2)}, u32[]{:S(2)}) collective-permute-start(bf16[256,1024]{1,0:T(8,128)(2,1)S(1)} %get-tuple-element.50), channel_id=1, source_target_pairs={{0,3},{1,0},{2,1},{3,2},{4,7},{5,4},{6,5},{7,6},{8,11},{9,8},{10,9... | collective-permute-start | bytes 1572872 | tf_op jit(solution)/shard_map/ppermute | solution.py:17
  55.7 24.6 %collective-permute-start.4 = (bf16[256,1024]{1,0:T(8,128)(2,1)S(1)}, bf16[256,1024]{1,0:T(8,128)(2,1)S(1)}, u32[]{:S(2)}, u32[]{:S(2)}) collective-permute-start(bf16[256,1024]{1,0:T(8,128)(2,1)S(1)} %get-tuple-element.51), channel_id=1, source_target_pairs={{0,1},{1,2},{2,3},{3,0},{4,5},{5,6},{6,7},{7,4},{8,9},{9,10},{10,1... | collective-permute-start | bytes 1572872 | tf_op jit(solution)/shard_map/ppermute | solution.py:17
  59.9 20.4 %copy-start.5 = (bf16[1024,768]{1,0:T(8,128)(2,1)S(1)}, bf16[1024,768]{1,0:T(8,128)(2,1)}, u32[]{:S(2)}) copy-start(bf16[1024,768]{1,0:T(8,128)(2,1)} %pad_maximum_fusion.1) | copy-start | bytes 4718596
  68.5 20.3 %collective-permute-start.7 = (bf16[256,1024]{1,0:T(8,128)(2,1)S(1)}, bf16[256,1024]{1,0:T(8,128)(2,1)S(1)}, u32[]{:S(2)}, u32[]{:S(2)}) collective-permute-start(bf16[256,1024]{1,0:T(8,128)(2,1)S(1)} %collective-permute-done.3), channel_id=1, source_target_pairs={{0,1},{1,2},{2,3},{3,0},{4,5},{5,6},{6,7},{7,4},{8,9},{9,10},{10,1... | collective-permute-start | bytes 1572872 | tf_op jit(solution)/shard_map/ppermute | solution.py:17
  68.5 20.3 %collective-permute-start.8 = (bf16[256,1024]{1,0:T(8,128)(2,1)S(1)}, bf16[256,1024]{1,0:T(8,128)(2,1)S(1)}, u32[]{:S(2)}, u32[]{:S(2)}) collective-permute-start(bf16[256,1024]{1,0:T(8,128)(2,1)S(1)} %collective-permute-done.6), channel_id=1, source_target_pairs={{0,3},{1,0},{2,1},{3,2},{4,7},{5,4},{6,5},{7,6},{8,11},{9,8},{10,9... | collective-permute-start | bytes 1572872 | tf_op jit(solution)/shard_map/ppermute | solution.py:17
  90.1 17.1 %collective-permute-start.11 = (bf16[256,384]{1,0:T(8,128)(2,1)S(1)}, bf16[256,384]{1,0:T(8,128)(2,1)S(1)}, u32[]{:S(2)}, u32[]{:S(2)}) collective-permute-start(bf16[256,384]{1,0:T(8,128)(2,1)S(1)} %get-tuple-element.52), channel_id=1, source_target_pairs={{0,3},{1,0},{2,1},{3,2},{4,7},{5,4},{6,5},{7,6},{8,11},{9,8},{10,9... | collective-permute-start | bytes 589832 | tf_op jit(solution)/shard_map/ppermute | solution.py:17
  93.1 9.0 %collective-permute-start.9 = (bf16[256,384]{1,0:T(8,128)(2,1)S(1)}, bf16[256,384]{1,0:T(8,128)(2,1)S(1)}, u32[]{:S(2)}, u32[]{:S(2)}) collective-permute-start(bf16[256,384]{1,0:T(8,128)(2,1)S(1)} %get-tuple-element.52), channel_id=1, source_target_pairs={{0,1},{1,2},{2,3},{3,0},{4,5},{5,6},{6,7},{7,4},{8,9},{9,10},{10,1... | collective-permute-start | bytes 589832 | tf_op jit(solution)/shard_map/ppermute | solution.py:17
  93.1 9.0 %collective-permute-start.12 = (bf16[256,384]{1,0:T(8,128)(2,1)S(1)}, bf16[256,384]{1,0:T(8,128)(2,1)S(1)}, u32[]{:S(2)}, u32[]{:S(2)}) collective-permute-start(bf16[256,384]{1,0:T(8,128)(2,1)S(1)} %get-tuple-element.53), channel_id=1, source_target_pairs={{0,3},{1,0},{2,1},{3,2},{4,7},{5,4},{6,5},{7,6},{8,11},{9,8},{10,9... | collective-permute-start | bytes 589832 | tf_op jit(solution)/shard_map/ppermute | solution.py:17
  96.3 9.0 %collective-permute-start.10 = (bf16[256,384]{1,0:T(8,128)(2,1)S(1)}, bf16[256,384]{1,0:T(8,128)(2,1)S(1)}, u32[]{:S(2)}, u32[]{:S(2)}) collective-permute-start(bf16[256,384]{1,0:T(8,128)(2,1)S(1)} %get-tuple-element.53), channel_id=1, source_target_pairs={{0,1},{1,2},{2,3},{3,0},{4,5},{5,6},{6,7},{7,4},{8,9},{9,10},{10,1... | collective-permute-start | bytes 589832 | tf_op jit(solution)/shard_map/ppermute | solution.py:17
  102.1 7.0 %collective-permute-start.13 = (bf16[256,384]{1,0:T(8,128)(2,1)S(1)}, bf16[256,384]{1,0:T(8,128)(2,1)S(1)}, u32[]{:S(2)}, u32[]{:S(2)}) collective-permute-start(bf16[256,384]{1,0:T(8,128)(2,1)S(1)} %collective-permute-done.9), channel_id=1, source_target_pairs={{0,1},{1,2},{2,3},{3,0},{4,5},{5,6},{6,7},{7,4},{8,9},{9,10},{10,1... | collective-permute-start | bytes 589832 | tf_op jit(solution)/shard_map/ppermute | solution.py:17
  102.1 7.0 %collective-permute-start.14 = (bf16[256,384]{1,0:T(8,128)(2,1)S(1)}, bf16[256,384]{1,0:T(8,128)(2,1)S(1)}, u32[]{:S(2)}, u32[]{:S(2)}) collective-permute-start(bf16[256,384]{1,0:T(8,128)(2,1)S(1)} %collective-permute-done.12), channel_id=1, source_target_pairs={{0,3},{1,0},{2,1},{3,2},{4,7},{5,4},{6,5},{7,6},{8,11},{9,8},{10,9... | collective-permute-start | bytes 589832 | tf_op jit(solution)/shard_map/ppermute | solution.py:17
  110.8 8.0 %copy-start.9 = (bf16[32,2048]{1,0:T(8,128)(2,1)S(1)}, bf16[32,2048]{1,0:T(8,128)(2,1)}, u32[]{:S(2)}) copy-start(bf16[32,2048]{1,0:T(8,128)(2,1)} %param.23) | copy-start | bytes 393220
  110.8 8.0 %copy-start.14 = (bf16[1,128,128]{2,1,0:T(8,128)(2,1)S(1)}, bf16[1,128,128]{2,1,0:T(8,128)(2,1)}, u32[]{:S(2)}) copy-start(bf16[1,128,128]{2,1,0:T(8,128)(2,1)} %param.24) | copy-start | bytes 98308
  110.8 8.3 %copy-start.12 = (f32[32,32]{1,0:T(8,128)S(1)}, f32[32,32]{1,0:T(8,128)}, u32[]{:S(2)}) copy-start(f32[32,32]{1,0:T(8,128)} %shard_map.166) | copy-start | bytes 12292
  110.8 36.4 %copy-start.2 = (bf16[32,1024]{1,0:T(8,128)(2,1)S(1)}, bf16[32,1024]{1,0:T(8,128)(2,1)}, u32[]{:S(2)}) copy-start(bf16[32,1024]{1,0:T(8,128)(2,1)} %hidden_ref.1) | copy-start | bytes 196612
  110.9 36.1 %all-to-all-start.1 = ((bf16[64,8,1024]{2,1,0:T(8,128)(2,1)}), bf16[64,8,1024]{2,1,0:T(8,128)(2,1)S(1)}, u32[]{:S(2)}, u32[]{:S(2)}) async-start(bf16[64,8,1024]{2,1,0:T(8,128)(2,1)} %fusion), calls=%async_computation.1 | async-start | bytes 2097152 | tf_op jit(solution)/shard_map/all_to_all | solution.py:243
  147.0 11.9 %copy-start.11 = (f32[4096]{0:T(1024)S(1)}, f32[4096]{0:T(1024)}, u32[]{:S(2)}) copy-start(f32[4096]{0:T(1024)} %param.20) | copy-start | bytes 49156
  147.3 11.9 %copy-start.10 = (bf16[32,1024]{1,0:T(8,128)(2,1)}, bf16[32,1024]{1,0:T(8,128)(2,1)S(1)}, u32[]{:S(2)}) copy-start(bf16[32,1024]{1,0:T(8,128)(2,1)S(1)} %fusion.45) | copy-start | bytes 196612
  148.1 11.2 %copy-start.8 = (bf16[4096,128]{1,0:T(8,128)(2,1)S(1)}, bf16[4096,128]{1,0:T(8,128)(2,1)}, u32[]{:S(2)}) copy-start(bf16[4096,128]{1,0:T(8,128)(2,1)} %param.21) | copy-start | bytes 3145732
  148.1 10.5 %all-to-all-start.2 = ((bf16[4,32,1024]{2,1,0:T(8,128)(2,1)}), bf16[4,32,1024]{2,1,0:T(8,128)(2,1)S(1)}, u32[]{:S(2)}, u32[]{:S(2)}) async-start(bf16[4,32,1024]{2,1,0:T(8,128)(2,1)} %broadcast_in_dim.36), calls=%async_computation.2 | async-start | bytes 524288 | tf_op jit(solution)/shard_map/all_to_all | solution.py:109
  158.9 1.4 copy-start.16
  159.2 1.7 %copy-start.15 = (bf16[32,128]{1,0:T(8,128)(2,1)}, bf16[32,128]{1,0:T(8,128)(2,1)S(1)}, u32[]{:S(2)}) copy-start(bf16[32,128]{1,0:T(8,128)(2,1)S(1)} %convolution_convert_fusion) | copy-start | bytes 24580
  159.6 2.1 %copy-start.13 = (bf16[32,128]{1,0:T(8,128)(2,1)}, bf16[32,128]{1,0:T(8,128)(2,1)S(1)}, u32[]{:S(2)}) copy-start(bf16[32,128]{1,0:T(8,128)(2,1)S(1)} %convolution_convert_fusion.1) | copy-start | bytes 24580

commit v4 on v3

--- a/solution.py
+++ b/solution.py
@@ -238,7 +238,7 @@
         products = summed_products(gathered_ring(rows), both_weights)
         gate_act, upward = products[:, :hidden_units], products[:, hidden_units:]
         active = (jax.nn.silu(gate_act) * upward).astype(jnp.bfloat16)
-        made = summed_products(gathered_ring(active), down_blocks).astype(jnp.bfloat16)
+        made = summed_products([active, *sent_around([active] * 3)], down_blocks).astype(jnp.bfloat16)
         returned.append(
             lax.all_to_all(
                 made.reshape(expert_count, chunk, column_count), "dp", split_axis=0, concat_axis=0, tiled=True

time: 162 us -> 165 us (1.019)
  waiting for transfers between devices: 76.6 us -> 83.7 us
  starting transfers between devices: 46.6 us -> 42.5 us
    ppermute x15 -> x12, waiting for transfers between devices: 38.7 us -> 45.9 us  [shifted(): lax.ppermute(value, 'tp', [(i, (i + step) % size) for i in range(size)])]
    ppermute x15 -> x12, starting transfers between devices: 23.3 us -> 18.3 us  [shifted(): lax.ppermute(value, 'tp', [(i, (i + step) % size) for i in range(size)])]
  transfers between devices with their start and end apart: 18 -> 15, of which waited for: 10 -> 10; matrix products, arithmetic and copies ran while one was open for 13% -> 13% of each run, Pallas kernels for 2% -> 2%
where the time goes in v4:
time: 165 us
  waiting for transfers between devices  83.7 us (51%)
  starting transfers between devices  42.5 us (26%)
  matrix products  15.3 us (9%)
  local copies, waits for them, and re-layouts  13.6 us (8%)
  other arithmetic  4.83 us (3%)
  Pallas kernels  2.96 us (2%)
  between operations  1.7 us (1%)
    ppermute x12, waiting for transfers between devices, shifted(): lax.ppermute(value, 'tp', [(i, (i + step) % size) for i in range(size)])  45.9 us
    all_to_all x1, waiting for transfers between devices, on_device(): lax.all_to_all(made.reshape(expert_count, chunk, column_count), 'dp', spl...  27.4 us
    ppermute x12, starting transfers between devices, shifted(): lax.ppermute(value, 'tp', [(i, (i + step) % size) for i in range(size)])  18.3 us
    all_to_all x1, starting transfers between devices, on_device(): lax.all_to_all(outgoing, 'dp', split_axis=0, concat_axis=0, tiled=True)  12.2 us
    dot_general x6, matrix products, summed_products(): total = total + jnp.dot(block, weight, preferred_element_type=jnp.float32)  8.43 us
    dynamic_slice x3, local copies, waits for them, and re-layouts, around(): lax.dynamic_slice_in_dim(value, (index + step) % count * size, size, dim)  8.35 us
    all_to_all x1, starting transfers between devices, on_device(): lax.all_to_all(made.reshape(expert_count, chunk, column_count), 'dp', spl...  8.02 us
    all_to_all x1, waiting for transfers between devices, copy_for_each(): return lax.all_to_all(copies, axis, split_axis=0, concat_axis=0, tiled=True)  6.3 us
  transfers between devices with their start and end apart: 15, of which 10 were waited for; matrix products, arithmetic and copies ran while one was open for 13% of the time, Pallas kernels for 2%

profile of v4, /device:TPU:2, one launch (start us, length us, event | category | flops | bytes accessed | tf_op | source)
XLA Modules:
  0.0 164.7 jit_solution(5194772354136894646)
XLA Ops:
  0.7 2.3 %dynamic-slice_bitcast_fusion.10 = bf16[384,1024]{1,0:T(8,128)(2,1)} fusion(bf16[1,384,4096]{2,1,0:T(8,128)(2,1)} %param.19, s32[]{:T(128)S(6)} %select_n.67), kind=kLoop, calls=%fused_computation.56 | loop fusion | bytes 1572868 | tf_op jit(solution)/shard_map/dynamic_slice | solution.py:84
  2.9 3.2 %collective-permute-start.2 = (bf16[384,1024]{1,0:T(8,128)(2,1)}, bf16[384,1024]{1,0:T(8,128)(2,1)S(1)}, u32[]{:S(2)}, u32[]{:S(2)}) collective-permute-start(bf16[384,1024]{1,0:T(8,128)(2,1)} %dynamic-slice_bitcast_fusion.10), channel_id=1, source_target_pairs={{0,2},{1,3},{2,0},{3,1},{4,6},{5,7},{6,4},{7,5},{8,10},{9,11},{10,... | collective-permute-start | bytes 2359304 | tf_op jit(solution)/shard_map/ppermute | solution.py:17
  6.1 0.8 copy-done.1
  7.0 0.7 copy-done.3
  7.6 0.7 copy-done.4
  8.3 1.7 %shard_map.165 = (bf16[512,1024]{1,0:T(8,128)(2,1)}, bf16[512,64]{1,0:T(8,128)(2,1)S(1)}) custom-call(s32[8,32]{1,0:T(8,128)S(1)} %bitcast.132, f32[8,32]{1,0:T(8,128)S(1)} %bitcast.133, bf16[32,1024]{1,0:T(8,128)(2,1)S(1)} %copy-done.1), custom_call_target="tpu_custom_call" | custom-call | flops 67108864 | bytes 1572864 | tf_op jit(solution)/shard_map/pallas_call | solution.py:69
  10.0 12.2 %all-to-all-start = ((bf16[64,8,1024]{2,1,0:T(8,128)(2,1)}), bf16[64,8,1024]{2,1,0:T(8,128)(2,1)}, u32[]{:S(2)}, u32[]{:S(2)}) async-start(bf16[64,8,1024]{2,1,0:T(8,128)(2,1)} %bitcast.3), calls=%async_computation | async-start | bytes 2097152 | tf_op jit(solution)/shard_map/all_to_all | solution.py:227
  22.3 2.7 %dynamic-slice_bitcast_fusion.8 = (bf16[384,1024]{1,0:T(8,128)(2,1)}, bf16[384,1024]{1,0:T(8,128)(2,1)}) fusion(bf16[1,384,4096]{2,1,0:T(8,128)(2,1)} %param.19, s32[]{:T(128)S(6)} %select_n.71, s32[]{:T(128)S(6)} %select_n.69), kind=kLoop, calls=%fused_computation.54 | loop fusion | bytes 3145736 | tf_op jit(solution)/shard_map/dynamic_slice | solution.py:84
  24.9 1.1 collective-permute-start.1
  26.0 1.0 collective-permute-start
  26.9 3.4 %dynamic-slice_bitcast_fusion = (bf16[1024,384]{1,0:T(8,128)(2,1)S(1)}, bf16[1024,384]{1,0:T(8,128)(2,1)S(1)}, bf16[1024,384]{1,0:T(8,128)(2,1)S(1)}, bf16[1024,...) fusion(bf16[1,4096,384]{2,1,0:T(8,128)(2,1)} %param.18, ...), kind=kLoop, calls=%fused_computation.46 | loop fusion | bytes 12582928 | tf_op jit(solution)/shard_map/dynamic_slice | solution.py:84
  30.5 1.3 pad_maximum_fusion.1
  31.8 1.3 pad_maximum_fusion
  33.1 1.3 pad_maximum_fusion.2
  34.4 1.3 shard_map.166
  35.7 9.2 %collective-permute-done.1 = bf16[384,1024]{1,0:T(8,128)(2,1)} collective-permute-done((bf16[384,1024]{1,0:T(8,128)(2,1)}, bf16[384,1024]{1,0:T(8,128)(2,1)}, u32[]{:S(2)}, u32[]{:S(2)}) %collective-permute-start.1) | collective-permute-done | bytes 786464 | tf_op jit(solution)/shard_map/ppermute | solution.py:17
  44.8 2.0 %collective-permute-done = bf16[384,1024]{1,0:T(8,128)(2,1)} collective-permute-done((bf16[384,1024]{1,0:T(8,128)(2,1)}, bf16[384,1024]{1,0:T(8,128)(2,1)}, u32[]{:S(2)}, u32[]{:S(2)}) %collective-permute-start) | collective-permute-done | bytes 786464 | tf_op jit(solution)/shard_map/ppermute | solution.py:17
  46.8 4.1 %all-to-all-done = bf16[64,8,1024]{2,1,0:T(8,128)(2,1)} async-done(((bf16[64,8,1024]{2,1,0:T(8,128)(2,1)}), bf16[64,8,1024]{2,1,0:T(8,128)(2,1)}, u32[]{:S(2)}, u32[]{:S(2)}) %all-to-all-start) | async-done | bytes 1048608 | tf_op jit(solution)/shard_map/all_to_all | solution.py:227
  50.9 1.4 slice_bitcast_fusion.1
  52.3 0.8 collective-permute-start.3
  53.1 2.6 %collective-permute-start.6 = (bf16[256,1024]{1,0:T(8,128)(2,1)S(1)}, bf16[256,1024]{1,0:T(8,128)(2,1)S(1)}, u32[]{:S(2)}, u32[]{:S(2)}) collective-permute-start(bf16[256,1024]{1,0:T(8,128)(2,1)S(1)} %get-tuple-element.51), channel_id=1, source_target_pairs={{0,3},{1,0},{2,1},{3,2},{4,7},{5,4},{6,5},{7,6},{8,11},{9,8},{10,9... | collective-permute-start | bytes 1572872 | tf_op jit(solution)/shard_map/ppermute | solution.py:17
  55.7 2.0 %collective-permute-start.4 = (bf16[256,1024]{1,0:T(8,128)(2,1)S(1)}, bf16[256,1024]{1,0:T(8,128)(2,1)S(1)}, u32[]{:S(2)}, u32[]{:S(2)}) collective-permute-start(bf16[256,1024]{1,0:T(8,128)(2,1)S(1)} %get-tuple-element.51), channel_id=1, source_target_pairs={{0,1},{1,2},{2,3},{3,0},{4,5},{5,6},{6,7},{7,4},{8,9},{9,10},{10,1... | collective-permute-start | bytes 1572872 | tf_op jit(solution)/shard_map/ppermute | solution.py:17
  57.7 2.2 %fusion.22 = f32[512,768]{1,0:T(8,128)S(1)} fusion(bf16[1024,768]{1,0:T(8,128)(2,1)S(1)} %copy-done.7, bf16[64,8,1024]{2,1,0:T(8,128)(2,1)} %all-to-all-done), kind=kOutput, calls=%fused_computation.39 | convolution fusion | flops 805306368 | bytes 4194304 | tf_op jit(solution)/shard_map/dot_general | solution.py:95
  59.9 8.6 %collective-permute-done.3 = bf16[256,1024]{1,0:T(8,128)(2,1)S(1)} collective-permute-done((bf16[256,1024]{1,0:T(8,128)(2,1)S(1)}, bf16[256,1024]{1,0:T(8,128)(2,1)S(1)}, u32[]{:S(2)}, u32[]{:S(2)}) %collective-permute-start.3) | collective-permute-done | bytes 524320 | tf_op jit(solution)/shard_map/ppermute | solution.py:17
  68.5 3.2 %collective-permute-start.8 = (bf16[256,1024]{1,0:T(8,128)(2,1)S(1)}, bf16[256,1024]{1,0:T(8,128)(2,1)S(1)}, u32[]{:S(2)}, u32[]{:S(2)}) collective-permute-start(bf16[256,1024]{1,0:T(8,128)(2,1)S(1)} %collective-permute-done.6), channel_id=1, source_target_pairs={{0,3},{1,0},{2,1},{3,2},{4,7},{5,4},{6,5},{7,6},{8,11},{9,8},{10,9... | collective-permute-start | bytes 1572872 | tf_op jit(solution)/shard_map/ppermute | solution.py:17
  71.7 7.5 %collective-permute-done.5 = bf16[256,1024]{1,0:T(8,128)(2,1)S(1)} collective-permute-done((bf16[256,1024]{1,0:T(8,128)(2,1)S(1)}, bf16[256,1024]{1,0:T(8,128)(2,1)S(1)}, u32[]{:S(2)}, u32[]{:S(2)}) %collective-permute-start.5) | collective-permute-done | bytes 524320 | tf_op jit(solution)/shard_map/ppermute | solution.py:17
  79.3 1.0 fusion.13
  80.3 1.0 fusion.9
  81.3 7.5 %collective-permute-done.7 = bf16[256,1024]{1,0:T(8,128)(2,1)S(1)} collective-permute-done((bf16[256,1024]{1,0:T(8,128)(2,1)S(1)}, bf16[256,1024]{1,0:T(8,128)(2,1)S(1)}, u32[]{:S(2)}, u32[]{:S(2)}) %collective-permute-start.7) | collective-permute-done | bytes 524320 | tf_op jit(solution)/shard_map/ppermute | solution.py:17
  88.8 1.0 add_add_fusion
  90.1 4.4 %collective-permute-start.11 = (bf16[512,384]{1,0:T(8,128)(2,1)S(1)}, bf16[512,384]{1,0:T(8,128)(2,1)S(1)}, u32[]{:S(2)}, u32[]{:S(2)}) collective-permute-start(bf16[512,384]{1,0:T(8,128)(2,1)S(1)} %fusion.24), channel_id=1, source_target_pairs={{0,2},{1,3},{2,0},{3,1},{4,6},{5,7},{6,4},{7,5},{8,10},{9,11},{10,... | collective-permute-start | bytes 1179656 | tf_op jit(solution)/shard_map/ppermute | solution.py:17
  94.5 1.8 %fusion.25 = f32[512,1024]{1,0:T(8,128)S(1)} fusion(bf16[512,384]{1,0:T(8,128)(2,1)S(1)} %fusion.24, bf16[1,384,4096]{2,1,0:T(8,128)(2,1)} %param.19, s32[]{:T(128)S(6)} %select_n.73), kind=kOutput, calls=%fused_computation.43 | convolution fusion | flops 402653184 | bytes 3276804 | tf_op jit(solution)/shard_map/dot_general | solution.py:95
  96.4 6.4 %collective-permute-done.9 = bf16[512,384]{1,0:T(8,128)(2,1)S(1)} collective-permute-done((bf16[512,384]{1,0:T(8,128)(2,1)S(1)}, bf16[512,384]{1,0:T(8,128)(2,1)S(1)}, u32[]{:S(2)}, u32[]{:S(2)}) %collective-permute-start.9) | collective-permute-done | bytes 393248 | tf_op jit(solution)/shard_map/ppermute | solution.py:17
  102.7 1.8 %fusion.55 = f32[512,1024]{1,0:T(8,128)S(1)} fusion(bf16[512,384]{1,0:T(8,128)(2,1)S(1)} %collective-permute-done.9, bf16[384,1024]{1,0:T(8,128)(2,1)} %collective-permute-done), kind=kOutput, calls=%fused_computation.97 | convolution fusion | flops 402653184 | bytes 3276800 | tf_op jit(solution)/shard_map/dot_general | solution.py:97
  104.6 4.7 %collective-permute-done.10 = bf16[512,384]{1,0:T(8,128)(2,1)S(1)} collective-permute-done((bf16[512,384]{1,0:T(8,128)(2,1)S(1)}, bf16[512,384]{1,0:T(8,128)(2,1)S(1)}, u32[]{:S(2)}, u32[]{:S(2)}) %collective-permute-start.10) | collective-permute-done | bytes 393248 | tf_op jit(solution)/shard_map/ppermute | solution.py:17
  109.3 1.8 %fusion.56 = f32[512,1024]{1,0:T(8,128)S(1)} fusion(bf16[512,384]{1,0:T(8,128)(2,1)S(1)} %collective-permute-done.10, bf16[384,1024]{1,0:T(8,128)(2,1)} %collective-permute-done.1), kind=kOutput, calls=%fused_computation.98 | convolution fusion | flops 402653184 | bytes 3276800 | tf_op jit(solution)/shard_map/dot_general | solution.py:97
  111.2 1.8 %fusion.8 = bf16[64,8,1024]{2,1,0:T(8,128)(2,1)} fusion(f32[512,1024]{1,0:T(8,128)S(1)} %fusion.56, f32[512,1024]{1,0:T(8,128)S(1)} %fusion.25, f32[512,1024]{1,0:T(8,128)S(1)} %fusion.55, bf16[512,384]{1,0:T(8,128)(2,1)S(1)} %collective-permute-done.11, bf16[384,1024]{1,0:T(8,128)(2,1)S(1)} %collective-permute-done.2), kind=kOutput, calls=%fused_computation.25 | convolution fusion | flops 404750336 | bytes 8519680 | tf_op jit(solution)/shard_map/dot_general | solution.py:97
  112.9 8.0 %all-to-all-start.1 = ((bf16[64,8,1024]{2,1,0:T(8,128)(2,1)}), bf16[64,8,1024]{2,1,0:T(8,128)(2,1)S(1)}, u32[]{:S(2)}, u32[]{:S(2)}) async-start(bf16[64,8,1024]{2,1,0:T(8,128)(2,1)} %fusion.8), calls=%async_computation.1 | async-start | bytes 2097152 | tf_op jit(solution)/shard_map/all_to_all | solution.py:243
  122.3 27.4 %all-to-all-done.1 = bf16[64,8,1024]{2,1,0:T(8,128)(2,1)S(1)} async-done(((bf16[64,8,1024]{2,1,0:T(8,128)(2,1)}), bf16[64,8,1024]{2,1,0:T(8,128)(2,1)S(1)}, u32[]{:S(2)}, u32[]{:S(2)}) %all-to-all-start.1) | async-done | bytes 1048608 | tf_op jit(solution)/shard_map/all_to_all | solution.py:243
  149.8 0.3 fusion.20
  150.1 0.7 broadcast_in_dim.36
  150.9 4.0 %all-to-all-start.2 = ((bf16[4,32,1024]{2,1,0:T(8,128)(2,1)}), bf16[4,32,1024]{2,1,0:T(8,128)(2,1)S(1)}, u32[]{:S(2)}, u32[]{:S(2)}) async-start(bf16[4,32,1024]{2,1,0:T(8,128)(2,1)} %broadcast_in_dim.36), calls=%async_computation.2 | async-start | bytes 524288 | tf_op jit(solution)/shard_map/all_to_all | solution.py:109
  155.3 6.3 %all-to-all-done.2 = bf16[4,32,1024]{2,1,0:T(8,128)(2,1)S(1)} async-done(((bf16[4,32,1024]{2,1,0:T(8,128)(2,1)}), bf16[4,32,1024]{2,1,0:T(8,128)(2,1)S(1)}, u32[]{:S(2)}, u32[]{:S(2)}) %all-to-all-start.2) | async-done | bytes 262176 | tf_op jit(solution)/shard_map/all_to_all | solution.py:109
  161.9 0.3 convolution_convert_fusion
  162.3 0.3 convolution_convert_fusion.1
  162.6 0.3 fusion.54
  163.3 0.3 convolution_bitcast_fusion
  164.0 0.7 copy.50
  (59 shorter events, 2.6 us)
Async XLA Ops:
  0.6 161.2 %copy-start = (bf16[4096,128]{1,0:T(8,128)(2,1)S(1)}, bf16[4096,128]{1,0:T(8,128)(2,1)}, u32[]{:S(2)}) copy-start(bf16[4096,128]{1,0:T(8,128)(2,1)} %param.22) | copy-start | bytes 3145732
  2.9 31.5 %collective-permute-start.2 = (bf16[384,1024]{1,0:T(8,128)(2,1)}, bf16[384,1024]{1,0:T(8,128)(2,1)S(1)}, u32[]{:S(2)}, u32[]{:S(2)}) collective-permute-start(bf16[384,1024]{1,0:T(8,128)(2,1)} %dynamic-slice_bitcast_fusion.10), channel_id=1, source_target_pairs={{0,2},{1,3},{2,0},{3,1},{4,6},{5,7},{6,4},{7,5},{8,10},{9,11},{10,... | collective-permute-start | bytes 2359304 | tf_op jit(solution)/shard_map/ppermute | solution.py:17
  6.1 0.8 copy-start.1
  7.0 0.7 copy-start.3
  7.6 0.7 copy-start.4
  10.0 40.9 %all-to-all-start = ((bf16[64,8,1024]{2,1,0:T(8,128)(2,1)}), bf16[64,8,1024]{2,1,0:T(8,128)(2,1)}, u32[]{:S(2)}, u32[]{:S(2)}) async-start(bf16[64,8,1024]{2,1,0:T(8,128)(2,1)} %bitcast.3), calls=%async_computation | async-start | bytes 2097152 | tf_op jit(solution)/shard_map/all_to_all | solution.py:227
  24.9 19.9 %collective-permute-start.1 = (bf16[384,1024]{1,0:T(8,128)(2,1)}, bf16[384,1024]{1,0:T(8,128)(2,1)}, u32[]{:S(2)}, u32[]{:S(2)}) collective-permute-start(bf16[384,1024]{1,0:T(8,128)(2,1)} %get-tuple-element.48), channel_id=1, source_target_pairs={{0,3},{1,0},{2,1},{3,2},{4,7},{5,4},{6,5},{7,6},{8,11},{9,8},{10,9... | collective-permute-start | bytes 2359304 | tf_op jit(solution)/shard_map/ppermute | solution.py:17
  26.0 20.8 %collective-permute-start = (bf16[384,1024]{1,0:T(8,128)(2,1)}, bf16[384,1024]{1,0:T(8,128)(2,1)}, u32[]{:S(2)}, u32[]{:S(2)}) collective-permute-start(bf16[384,1024]{1,0:T(8,128)(2,1)} %get-tuple-element.49), channel_id=1, source_target_pairs={{0,1},{1,2},{2,3},{3,0},{4,5},{5,6},{6,7},{7,4},{8,9},{9,10},{10,1... | collective-permute-start | bytes 2359304 | tf_op jit(solution)/shard_map/ppermute | solution.py:17
  50.9 6.7 %copy-start.7 = (bf16[1024,768]{1,0:T(8,128)(2,1)S(1)}, bf16[1024,768]{1,0:T(8,128)(2,1)}, u32[]{:S(2)}) copy-start(bf16[1024,768]{1,0:T(8,128)(2,1)} %pad_maximum_fusion) | copy-start | bytes 4718596
  52.3 16.2 %collective-permute-start.3 = (bf16[256,1024]{1,0:T(8,128)(2,1)S(1)}, bf16[256,1024]{1,0:T(8,128)(2,1)S(1)}, u32[]{:S(2)}, u32[]{:S(2)}) collective-permute-start(bf16[256,1024]{1,0:T(8,128)(2,1)S(1)} %get-tuple-element.50), channel_id=1, source_target_pairs={{0,1},{1,2},{2,3},{3,0},{4,5},{5,6},{6,7},{7,4},{8,9},{9,10},{10,1... | collective-permute-start | bytes 1572872 | tf_op jit(solution)/shard_map/ppermute | solution.py:17
  53.1 26.2 %copy-start.6 = (bf16[1024,768]{1,0:T(8,128)(2,1)S(1)}, bf16[1024,768]{1,0:T(8,128)(2,1)}, u32[]{:S(2)}) copy-start(bf16[1024,768]{1,0:T(8,128)(2,1)} %pad_maximum_fusion.2) | copy-start | bytes 4718596
  53.1 15.4 %collective-permute-start.6 = (bf16[256,1024]{1,0:T(8,128)(2,1)S(1)}, bf16[256,1024]{1,0:T(8,128)(2,1)S(1)}, u32[]{:S(2)}, u32[]{:S(2)}) collective-permute-start(bf16[256,1024]{1,0:T(8,128)(2,1)S(1)} %get-tuple-element.51), channel_id=1, source_target_pairs={{0,3},{1,0},{2,1},{3,2},{4,7},{5,4},{6,5},{7,6},{8,11},{9,8},{10,9... | collective-permute-start | bytes 1572872 | tf_op jit(solution)/shard_map/ppermute | solution.py:17
  55.7 23.6 %collective-permute-start.5 = (bf16[256,1024]{1,0:T(8,128)(2,1)S(1)}, bf16[256,1024]{1,0:T(8,128)(2,1)S(1)}, u32[]{:S(2)}, u32[]{:S(2)}) collective-permute-start(bf16[256,1024]{1,0:T(8,128)(2,1)S(1)} %get-tuple-element.50), channel_id=1, source_target_pairs={{0,3},{1,0},{2,1},{3,2},{4,7},{5,4},{6,5},{7,6},{8,11},{9,8},{10,9... | collective-permute-start | bytes 1572872 | tf_op jit(solution)/shard_map/ppermute | solution.py:17
  55.7 24.6 %collective-permute-start.4 = (bf16[256,1024]{1,0:T(8,128)(2,1)S(1)}, bf16[256,1024]{1,0:T(8,128)(2,1)S(1)}, u32[]{:S(2)}, u32[]{:S(2)}) collective-permute-start(bf16[256,1024]{1,0:T(8,128)(2,1)S(1)} %get-tuple-element.51), channel_id=1, source_target_pairs={{0,1},{1,2},{2,3},{3,0},{4,5},{5,6},{6,7},{7,4},{8,9},{9,10},{10,1... | collective-permute-start | bytes 1572872 | tf_op jit(solution)/shard_map/ppermute | solution.py:17
  59.9 20.4 %copy-start.5 = (bf16[1024,768]{1,0:T(8,128)(2,1)S(1)}, bf16[1024,768]{1,0:T(8,128)(2,1)}, u32[]{:S(2)}) copy-start(bf16[1024,768]{1,0:T(8,128)(2,1)} %pad_maximum_fusion.1) | copy-start | bytes 4718596
  68.5 20.3 %collective-permute-start.7 = (bf16[256,1024]{1,0:T(8,128)(2,1)S(1)}, bf16[256,1024]{1,0:T(8,128)(2,1)S(1)}, u32[]{:S(2)}, u32[]{:S(2)}) collective-permute-start(bf16[256,1024]{1,0:T(8,128)(2,1)S(1)} %collective-permute-done.3), channel_id=1, source_target_pairs={{0,1},{1,2},{2,3},{3,0},{4,5},{5,6},{6,7},{7,4},{8,9},{9,10},{10,1... | collective-permute-start | bytes 1572872 | tf_op jit(solution)/shard_map/ppermute | solution.py:17
  68.5 20.3 %collective-permute-start.8 = (bf16[256,1024]{1,0:T(8,128)(2,1)S(1)}, bf16[256,1024]{1,0:T(8,128)(2,1)S(1)}, u32[]{:S(2)}, u32[]{:S(2)}) collective-permute-start(bf16[256,1024]{1,0:T(8,128)(2,1)S(1)} %collective-permute-done.6), channel_id=1, source_target_pairs={{0,3},{1,0},{2,1},{3,2},{4,7},{5,4},{6,5},{7,6},{8,11},{9,8},{10,9... | collective-permute-start | bytes 1572872 | tf_op jit(solution)/shard_map/ppermute | solution.py:17
  90.0 12.7 %collective-permute-start.9 = (bf16[512,384]{1,0:T(8,128)(2,1)S(1)}, bf16[512,384]{1,0:T(8,128)(2,1)S(1)}, u32[]{:S(2)}, u32[]{:S(2)}) collective-permute-start(bf16[512,384]{1,0:T(8,128)(2,1)S(1)} %fusion.24), channel_id=1, source_target_pairs={{0,1},{1,2},{2,3},{3,0},{4,5},{5,6},{6,7},{7,4},{8,9},{9,10},{10,1... | collective-permute-start | bytes 1179656 | tf_op jit(solution)/shard_map/ppermute | solution.py:17
  90.1 21.0 %collective-permute-start.11 = (bf16[512,384]{1,0:T(8,128)(2,1)S(1)}, bf16[512,384]{1,0:T(8,128)(2,1)S(1)}, u32[]{:S(2)}, u32[]{:S(2)}) collective-permute-start(bf16[512,384]{1,0:T(8,128)(2,1)S(1)} %fusion.24), channel_id=1, source_target_pairs={{0,2},{1,3},{2,0},{3,1},{4,6},{5,7},{6,4},{7,5},{8,10},{9,11},{10,... | collective-permute-start | bytes 1179656 | tf_op jit(solution)/shard_map/ppermute | solution.py:17
  94.5 14.8 %collective-permute-start.10 = (bf16[512,384]{1,0:T(8,128)(2,1)S(1)}, bf16[512,384]{1,0:T(8,128)(2,1)S(1)}, u32[]{:S(2)}, u32[]{:S(2)}) collective-permute-start(bf16[512,384]{1,0:T(8,128)(2,1)S(1)} %fusion.24), channel_id=1, source_target_pairs={{0,3},{1,0},{2,1},{3,2},{4,7},{5,4},{6,5},{7,6},{8,11},{9,8},{10,9... | collective-permute-start | bytes 1179656 | tf_op jit(solution)/shard_map/ppermute | solution.py:17
  112.9 8.7 %copy-start.9 = (bf16[32,2048]{1,0:T(8,128)(2,1)S(1)}, bf16[32,2048]{1,0:T(8,128)(2,1)}, u32[]{:S(2)}) copy-start(bf16[32,2048]{1,0:T(8,128)(2,1)} %param.23) | copy-start | bytes 393220
  112.9 8.7 %copy-start.14 = (bf16[1,128,128]{2,1,0:T(8,128)(2,1)S(1)}, bf16[1,128,128]{2,1,0:T(8,128)(2,1)}, u32[]{:S(2)}) copy-start(bf16[1,128,128]{2,1,0:T(8,128)(2,1)} %param.24) | copy-start | bytes 98308
  112.9 9.0 %copy-start.12 = (f32[32,32]{1,0:T(8,128)S(1)}, f32[32,32]{1,0:T(8,128)}, u32[]{:S(2)}) copy-start(f32[32,32]{1,0:T(8,128)} %shard_map.166) | copy-start | bytes 12292
  112.9 37.1 %copy-start.2 = (bf16[32,1024]{1,0:T(8,128)(2,1)S(1)}, bf16[32,1024]{1,0:T(8,128)(2,1)}, u32[]{:S(2)}) copy-start(bf16[32,1024]{1,0:T(8,128)(2,1)} %hidden_ref.1) | copy-start | bytes 196612
  112.9 36.8 %all-to-all-start.1 = ((bf16[64,8,1024]{2,1,0:T(8,128)(2,1)}), bf16[64,8,1024]{2,1,0:T(8,128)(2,1)S(1)}, u32[]{:S(2)}, u32[]{:S(2)}) async-start(bf16[64,8,1024]{2,1,0:T(8,128)(2,1)} %fusion.8), calls=%async_computation.1 | async-start | bytes 2097152 | tf_op jit(solution)/shard_map/all_to_all | solution.py:243
  149.8 12.1 %copy-start.11 = (f32[4096]{0:T(1024)S(1)}, f32[4096]{0:T(1024)}, u32[]{:S(2)}) copy-start(f32[4096]{0:T(1024)} %param.20) | copy-start | bytes 49156
  150.1 12.1 %copy-start.10 = (bf16[32,1024]{1,0:T(8,128)(2,1)}, bf16[32,1024]{1,0:T(8,128)(2,1)S(1)}, u32[]{:S(2)}) copy-start(bf16[32,1024]{1,0:T(8,128)(2,1)S(1)} %fusion.34) | copy-start | bytes 196612
  150.9 11.4 %copy-start.8 = (bf16[4096,128]{1,0:T(8,128)(2,1)S(1)}, bf16[4096,128]{1,0:T(8,128)(2,1)}, u32[]{:S(2)}) copy-start(bf16[4096,128]{1,0:T(8,128)(2,1)} %param.21) | copy-start | bytes 3145732
  150.9 10.7 %all-to-all-start.2 = ((bf16[4,32,1024]{2,1,0:T(8,128)(2,1)}), bf16[4,32,1024]{2,1,0:T(8,128)(2,1)S(1)}, u32[]{:S(2)}, u32[]{:S(2)}) async-start(bf16[4,32,1024]{2,1,0:T(8,128)(2,1)} %broadcast_in_dim.36), calls=%async_computation.2 | async-start | bytes 524288 | tf_op jit(solution)/shard_map/all_to_all | solution.py:109
  161.9 1.4 copy-start.16
  162.2 1.7 %copy-start.15 = (bf16[32,128]{1,0:T(8,128)(2,1)}, bf16[32,128]{1,0:T(8,128)(2,1)S(1)}, u32[]{:S(2)}) copy-start(bf16[32,128]{1,0:T(8,128)(2,1)S(1)} %convolution_convert_fusion) | copy-start | bytes 24580
  162.6 2.1 %copy-start.13 = (bf16[32,128]{1,0:T(8,128)(2,1)}, bf16[32,128]{1,0:T(8,128)(2,1)S(1)}, u32[]{:S(2)}) copy-start(bf16[32,128]{1,0:T(8,128)(2,1)S(1)} %convolution_convert_fusion.1) | copy-start | bytes 24580
